TPU v7x, 32 devices: a whole 2x2x4 slice. The times are simulated.
32 devices in a mesh: rep: 2 (over y), tp: 8 (over z, x), seq: 2 (over core).
Axes of the slice: x: 2, y: 2, z: 4, core: 2. Of those that a mesh axis runs over, the one named last changes fastest.
Arguments:
- gate_preact: bfloat16 [1536, 28672], P(('rep', 'seq'), 'tp'), parts along dimension 0, may hold values from -6 to 6
- up_preact: bfloat16 [1536, 28672], P(('rep', 'seq'), 'tp'), parts along dimension 0, may hold values from -6 to 6
- weight_codes: int32 [28672, 4096], P('tp'), may hold values from 0 to 255
- scale_down: float32 [8192], P('tp'), may hold values from 0.0006 to 0.0024
- grad_output: bfloat16 [1536, 8192], P(('rep', 'seq'), 'tp'), parts along dimension 0, may hold values from -6 to 6
Outputs:
- grad_gate: bfloat16 [1536, 28672], P(('rep', 'seq'), 'tp'), parts along dimension 0
- grad_up: bfloat16 [1536, 28672], P(('rep', 'seq'), 'tp'), parts along dimension 0
- scale_grad: float32 [16384], P(('rep', 'tp', 'seq')), parts along dimension 0
There are 2 independent parts, one for each index of `rep`. A program takes and returns all parts, laid end to end along the dimension named above; an argument that names none is the same for every part. Nothing has to cross between parts.
All inputs are finite; a program needn't handle non-finite values.
Results may differ from a plain program's by a relative error of at most 0.0051.
Values may be sent and summed in bfloat16 or wider, within the bound.
No kernel may reach another device: no remote copies, remote signals or barrier semaphores. Data moves between devices by JAX's collectives and lax.ppermute only.
A program may use at most 576 MiB of HBM per device.

v0:
```python
import jax
import jax.numpy as jnp
from jax import lax
from jax.sharding import PartitionSpec as P


def unpack(words):
    shifts = 4 * jnp.arange(2, dtype=jnp.int32)
    nibbles = jnp.bitwise_and(jnp.right_shift(words[:, :, None], shifts[None, None, :]), 15)
    return (nibbles.reshape(words.shape[0], words.shape[1] * 2) - 8).astype(jnp.bfloat16)


def per_device(gate_preact, up_preact, weight_codes, scale_down, grad_output):
    gate_vals = gate_preact.astype(jnp.float32)
    up_vals = up_preact.astype(jnp.float32)
    sigmoid_gate = jax.nn.sigmoid(gate_vals)
    hidden = (gate_vals * sigmoid_gate * up_vals).astype(jnp.bfloat16)
    centered = unpack(weight_codes)
    local_scaled = (grad_output.astype(jnp.float32) * scale_down[None, :]).astype(jnp.bfloat16)
    whole_grad = lax.all_gather(local_scaled, "tp", axis=1, tiled=True)
    grad_hidden = lax.dot_general(
        whole_grad, centered, (((1,), (1,)), ((), ())), preferred_element_type=jnp.float32
    )
    cross = lax.dot_general(
        hidden, whole_grad, (((0,), (0,)), ((), ())), preferred_element_type=jnp.float32
    )
    column_sums = jnp.sum(centered.astype(jnp.float32) * cross, axis=0)
    partial_sums = column_sums
    grad_hidden, partial_sums = (grad_hidden, partial_sums)
    grad_gate = (
        grad_hidden * up_vals * sigmoid_gate * (1.0 + gate_vals * (1.0 - sigmoid_gate))
    ).astype(jnp.bfloat16)
    grad_up = (grad_hidden * gate_vals * sigmoid_gate).astype(jnp.bfloat16)
    channel_sums = lax.psum_scatter(partial_sums, ("tp", "seq"), scatter_dimension=0, tiled=True)
    return (grad_gate, grad_up, channel_sums)


def solution(mesh):
    placed = (
        P(("rep", "seq"), "tp"),
        P(("rep", "seq"), "tp"),
        P("tp", None),
        P("tp"),
        P(("rep", "seq"), "tp"),
    )
    return jax.shard_map(
        per_device,
        mesh=mesh,
        in_specs=placed,
        out_specs=(P(("rep", "seq"), "tp"), P(("rep", "seq"), "tp"), P(("rep", "tp", "seq"))),
        check_vma=False,
    )
```

profile of v0, /device:TPU:0, one launch (start us, length us, event | category | flops | bytes accessed | tf_op | source)
XLA Modules:
  0.0 534.2 jit_solution(7853273767301638245)
XLA Ops:
  7.2 0.0 all-gather.2.cloned.1.call-start
  7.2 2.2 multiply_convert_fusion
  9.4 0.0 all-gather.2.cloned.1.call-update
  9.5 54.9 %copy.10 = s32[3584,4096]{0,1:T(8,128)} copy(s32[3584,4096]{1,0:T(8,128)} %param.7) | data formatting | bytes 117440512 | tf_op args[2]
  64.3 58.7 %shift_right_arithmetic.20 = s32[3584,4096,2]{0,2,1:T(2,128)} broadcast(s32[3584,4096]{0,1:T(8,128)} %copy.10), dimensions={0,1} | broadcast | bytes 176160768 | tf_op jit(solution)/shard_map/shift_right_arithmetic | solution.py:9
  123.0 132.8 %shift_right_arithmetic.21 = s32[3584,8192]{0,1:T(8,128)} reshape(s32[3584,4096,2]{0,2,1:T(2,128)} %shift_right_arithmetic.20) | data formatting | bytes 234881024 | tf_op jit(solution)/shard_map/shift_right_arithmetic | solution.py:9
  255.8 0.0 copy-start.1
  255.8 107.7 %copy.11 = s32[3584,8192]{1,0:T(8,128)} copy(s32[3584,8192]{0,1:T(8,128)} %shift_right_arithmetic.21) | data formatting | bytes 234881024 | tf_op jit(solution)/shard_map/shift_right_arithmetic | solution.py:9
  363.5 0.1 shift_right_arithmetic.22
  363.6 1.2 shift_right_arithmetic.23
  364.9 0.0 copy-done.1
  364.9 0.6 dynamic-slice
  366.1 0.0 copy-start
  366.1 0.0 all-gather.2.cloned.1.call-done
  366.1 54.5 %multiply_reduce_fusion = f32[8192]{0:T(1024)S(1)} fusion(bf16[384,8192]{1,0:T(8,128)(2,1)} %all-gather.2.cloned.1.call-done, s32[3584,8192]{1,0:T(8,128)} %copy.11, s32[8192]{0:T(1024)S(1)} %shift_right_arithmetic.23, bf16[384,3584]{1,0:T(8,128)(2,1)} %param.6, bf16[384,3584]{1,0:T(8,128)(2,1)} %param.5), kind=kOutput, calls=%fused_computation | convolution fusion | flops 22765101056 | bytes 129302528 | tf_op jit(solution)/shard_map/dot_general | solution.py:24
  420.7 62.7 %all-reduce = f32[8192]{0:T(1024)S(1)} all-reduce(f32[8192]{0:T(1024)S(1)} %multiply_reduce_fusion), channel_id=2, replica_groups=mesh['rep'=2,'tp'=8,'seq'=2] {'tp','seq'}, use_global_device_ids=true, to_apply=%region_1.0.clone | all-reduce | flops 8192 | bytes 65536
  483.4 0.7 dynamic-slice.1
  484.0 0.0 copy-done
  484.0 43.4 %fusion.10 = (bf16[384,3584]{1,0:T(8,128)(2,1)}, bf16[384,3584]{1,0:T(8,128)(2,1)}) fusion(bf16[384,3584]{1,0:T(8,128)(2,1)S(1)} %copy-done, bf16[384,3584]{1,0:T(8,128)(2,1)} %param.6, bf16[384,8192]{1,0:T(8,128)(2,1)} %all-gather.2.cloned.1.call-done, s32[3584,8192]{1,0:T(8,128)} %copy.11, s32[8192]{0:T(1024)S(1)} %shift_right_arithmetic.23), kind=kOutput, calls=%fused_computation.18 | convolution fusion | flops 22686662656 | bytes 134774784 | tf_op jit(solution)/shard_map/dot_general | solution.py:21
  (1 shorter events, 0.0 us)
Async XLA Ops:
  7.2 359.0 %all-gather.2.cloned.1.call-start = ((), (), s32[]{:S(2)}) async-start(), calls=%async_computation | async-start | bytes 7077888 | tf_op jit(solution)/shard_map/all_gather | solution.py:20
  255.8 109.1 %copy-start.1 = (u32[32]{0:T(128)S(1)}, u32[32]{0:T(128)}, u32[]{:S(2)}) copy-start(u32[32]{0:T(128)} %constant.13) | copy-start | bytes 388
  366.1 117.9 %copy-start = (bf16[384,3584]{1,0:T(8,128)(2,1)S(1)}, bf16[384,3584]{1,0:T(8,128)(2,1)}, u32[]{:S(2)}) copy-start(bf16[384,3584]{1,0:T(8,128)(2,1)} %param.5) | copy-start | bytes 8257540
Sparse Core Ops, SparseCore 0:
  10.8 101.7 all-gather.1
where the time goes:
time: 541 us; the launch traced here: 534 us
  local copies, waits for them, and re-layouts  357 us (66%)
  matrix products  97.9 us (18%)
  blocking collectives  62.7 us (12%)
  between operations  14.7 us (3%)
    shift_right_arithmetic x5, local copies, waits for them, and re-layouts, unpack(): jnp.right_shift(words[:, :, None], shifts[None, None, :])  301 us
    unnamed x1, blocking collectives  62.7 us
    unnamed x7, local copies, waits for them, and re-layouts  56.1 us
    dot_general x1, matrix products, per_device(): lax.dot_general(hidden, whole_grad, (((0,), (0,)), ((), ())), preferred_e...  54.5 us
    dot_general x1, matrix products, per_device(): lax.dot_general(whole_grad, centered, (((1,), (1,)), ((), ())), preferred...  43.4 us
  transfers between devices with their start and end apart: 1, of which 0 were waited for; matrix products, arithmetic and copies ran while one was open for 67% of the time, Pallas kernels for 0%

commit v1 on v0

v1 whole, which is shorter than its diff:
```python
import functools

import jax
import jax.numpy as jnp
from jax import lax
from jax.experimental import pallas as pl
from jax.experimental.pallas import tpu as pltpu
from jax.sharding import PartitionSpec as P

F32 = jnp.float32
BF16 = jnp.bfloat16
MIB = 1 << 20


def sigmoid(v):
    return 0.5 * jnp.tanh(0.5 * v) + 0.5


def nibbles(words):
    low = (jnp.bitwise_and(words, 15) - 8).astype(F32).astype(BF16)
    high = (jnp.right_shift(words, 4) - 8).astype(F32).astype(BF16)
    return jnp.concatenate([low, high], axis=1)


def cost(flops, bytes_accessed):
    return pl.CostEstimate(flops=int(flops), bytes_accessed=int(bytes_accessed), transcendentals=0)


def scale_kernel(grad_ref, scale_ref, out_ref):
    width = grad_ref.shape[1]
    half = width // 2
    scaled = (grad_ref[...].astype(F32) * scale_ref[...]).astype(BF16)
    source = lax.broadcasted_iota(jnp.int32, (256, 256), 0)
    target = lax.broadcasted_iota(jnp.int32, (256, 256), 1)
    wanted = jnp.where(target < 128, 2 * target, 2 * target - 255)
    pick = (source == wanted).astype(F32).astype(BF16)
    for b in range(width // 256):
        sorted_block = jnp.dot(scaled[:, 256 * b:256 * b + 256], pick, preferred_element_type=F32).astype(BF16)
        out_ref[:, 128 * b:128 * b + 128] = sorted_block[:, :128]
        out_ref[:, half + 128 * b:half + 128 * b + 128] = sorted_block[:, 128:]


def scale_call(grad, scale):
    rows, width = grad.shape
    return pl.pallas_call(
        scale_kernel,
        out_shape=jax.ShapeDtypeStruct((rows, width), BF16),
        name="scale",
        cost_estimate=cost(2 * rows * width * 256, 4 * rows * width),
    )(grad, scale.reshape(1, width))


def hidden_kernel(gate_ref, up_ref, out_ref):
    g = gate_ref[...].astype(F32)
    out_ref[...] = (g * sigmoid(g) * up_ref[...].astype(F32)).astype(BF16)


def hidden_call(gate, up):
    rows, units = gate.shape
    spec = pl.BlockSpec((rows, 512), lambda i: (0, i))
    return pl.pallas_call(
        hidden_kernel,
        grid=(units // 512,),
        in_specs=[spec, spec],
        out_specs=spec,
        out_shape=jax.ShapeDtypeStruct((rows, units), BF16),
        name="hidden",
        cost_estimate=cost(16 * rows * units, 6 * rows * units),
    )(gate, up)


def moments_kernel(order_ref, hidden_ref, words_ref, out_ref):
    shard_words = words_ref.shape[1]
    depth = words_ref.shape[0]
    step = pl.program_id(1)
    part = hidden_ref[:, pl.ds(pl.multiple_of(step * depth, depth), depth)]
    total = None
    for k in range(0, depth, 256):
        product = jnp.dot(part[:, k:k + 256], nibbles(words_ref[k:k + 256, :]), preferred_element_type=F32)
        total = product if total is None else total + product

    @pl.when(step == 0)
    def _():
        out_ref[0, 0] = total[:, :shard_words]
        out_ref[0, 1] = total[:, shard_words:]

    @pl.when(step > 0)
    def _():
        out_ref[0, 0] += total[:, :shard_words]
        out_ref[0, 1] += total[:, shard_words:]


def moments_call(order, hidden, words, first, n, shard_words):
    rows, units = hidden.shape
    depth = units // 2
    return pl.pallas_call(
        moments_kernel,
        grid_spec=pltpu.PrefetchScalarGridSpec(
            num_scalar_prefetch=1,
            grid=(n, units // depth),
            in_specs=[
                pl.BlockSpec((rows, units), lambda s, k, o: (0, 0)),
                pl.BlockSpec((depth, shard_words), lambda s, k, o: (k, o[first + s])),
            ],
            out_specs=pl.BlockSpec((1, 2, rows, shard_words), lambda s, k, o: (s, 0, 0, 0)),
        ),
        out_shape=jax.ShapeDtypeStruct((n, 2, rows, shard_words), F32),
        name="moments",
        compiler_params=pltpu.CompilerParams(vmem_limit_bytes=36 * MIB),
        cost_estimate=cost(4 * n * rows * units * shard_words, 4 * n * units * shard_words),
    )(order, hidden, words)


def back_kernel(n, first, order_ref, *refs):
    grads, words, moments = refs[:n], refs[n:2 * n], refs[2 * n:3 * n]
    out_ref, sums_ref = refs[-2:]
    step = pl.program_id(0)
    total = None if first else refs[3 * n][...]
    for s in range(n):
        product = lax.dot_general(
            grads[s][...], nibbles(words[s][...]), (((1,), (1,)), ((), ())), preferred_element_type=F32
        )
        total = product if total is None else total + product
    out_ref[...] = total
    add_sums(step, grads, moments, sums_ref)


def add_sums(step, grads, moments, sums_ref):
    rows = moments[0].shape[2]
    shard_words = moments[0].shape[3]

    @pl.when(step == 0)
    def _():
        sums_ref[...] = jnp.zeros_like(sums_ref)

    @pl.when(step * rows < grads[0].shape[0])
    def _():
        start = pl.ds(pl.multiple_of(step * rows, rows), rows)
        for s in range(len(grads)):
            for k in range(2):
                columns = slice(k * shard_words, (k + 1) * shard_words)
                terms = grads[s][start, columns].astype(F32) * moments[s][0, k]
                sums_ref[s, k:k + 1] += jnp.sum(terms, axis=0, keepdims=True)


def back_call(order, grads, shards, moments, words, total=None):
    n = len(grads)
    rows, width = grads[0].shape
    units = words.shape[0]
    shard_words = width // 2
    block = 512
    steps = units // block
    first = total is None
    sum_rows = 64
    last = rows // sum_rows - 1
    in_specs = [pl.BlockSpec((rows, width), lambda i, o: (0, 0)) for _ in range(n)]
    in_specs += [
        pl.BlockSpec((block, shard_words), functools.partial(lambda s, i, o: (i, o[s]), s)) for s in shards
    ]
    in_specs += [
        pl.BlockSpec(
            (1, 2, sum_rows, shard_words),
            functools.partial(lambda s, i, o: (s, 0, jnp.minimum(i, last), 0), s),
        )
        for _, s in moments
    ]
    operands = [order] + list(grads) + [words] * n + [m for m, _ in moments]
    aliases = {}
    if not first:
        in_specs.append(pl.BlockSpec((rows, block), lambda i, o: (0, i)))
        aliases = {len(operands): 0}
        operands.append(total)
    return pl.pallas_call(
        functools.partial(back_kernel, n, first),
        grid_spec=pltpu.PrefetchScalarGridSpec(
            num_scalar_prefetch=1,
            grid=(steps,),
            in_specs=in_specs,
            out_specs=[
                pl.BlockSpec((rows, block), lambda i, o: (0, i)),
                pl.BlockSpec((n, 2, shard_words), lambda i, o: (0, 0, 0)),
            ],
        ),
        out_shape=[
            jax.ShapeDtypeStruct((rows, units), F32),
            jax.ShapeDtypeStruct((n, 2, shard_words), F32),
        ],
        name="back",
        input_output_aliases=aliases,
        compiler_params=pltpu.CompilerParams(vmem_limit_bytes=40 * MIB),
        cost_estimate=cost(4 * n * rows * units * shard_words, 4 * n * units * shard_words),
    )(*operands)


def sums_kernel(grad_ref, moments_ref, out_ref):
    shard_words = moments_ref.shape[3]
    for k in range(2):
        columns = slice(k * shard_words, (k + 1) * shard_words)
        terms = grad_ref[:, columns].astype(F32) * moments_ref[0, k]
        out_ref[k:k + 1] = jnp.sum(terms, axis=0, keepdims=True)


def sums_call(grad, moments, place):
    rows, width = grad.shape
    return pl.pallas_call(
        sums_kernel,
        grid=(1,),
        in_specs=[
            pl.BlockSpec((rows, width), lambda i: (0, 0)),
            pl.BlockSpec((1, 2, rows, width // 2), lambda i: (place, 0, 0, 0)),
        ],
        out_specs=pl.BlockSpec((2, width // 2), lambda i: (0, 0)),
        out_shape=jax.ShapeDtypeStruct((2, width // 2), F32),
        name="sums",
        cost_estimate=cost(2 * rows * width, 6 * rows * width),
    )(grad, moments)


def tail_kernel(order_ref, grad_ref, words_ref, total_ref, gate_ref, up_ref, gate_out_ref, up_out_ref):
    grad_hidden = total_ref[...] + lax.dot_general(
        grad_ref[...], nibbles(words_ref[...]), (((1,), (1,)), ((), ())), preferred_element_type=F32
    )
    g = gate_ref[...].astype(F32)
    s = sigmoid(g)
    gate_out_ref[...] = (grad_hidden * up_ref[...].astype(F32) * s * (1.0 + g * (1.0 - s))).astype(BF16)
    up_out_ref[...] = (grad_hidden * g * s).astype(BF16)


def tail_call(order, grad, shard, words, total, gate, up):
    rows, width = grad.shape
    units = words.shape[0]
    block = 512
    wide = pl.BlockSpec((rows, block), lambda i, o: (0, i))
    return pl.pallas_call(
        tail_kernel,
        grid_spec=pltpu.PrefetchScalarGridSpec(
            num_scalar_prefetch=1,
            grid=(units // block,),
            in_specs=[
                pl.BlockSpec((rows, width), lambda i, o: (0, 0)),
                pl.BlockSpec((block, width // 2), lambda i, o: (i, o[shard])),
                wide,
                wide,
                wide,
            ],
            out_specs=[wide, wide],
        ),
        out_shape=[jax.ShapeDtypeStruct((rows, units), BF16)] * 2,
        name="tail",
        compiler_params=pltpu.CompilerParams(vmem_limit_bytes=32 * MIB),
        cost_estimate=cost(2 * rows * units * width, 2 * units * width + 12 * rows * units),
    )(order, grad, words, total, gate, up)


def by_ring(ring, gate, up, words, scale, grad):
    tp = 2 * ring
    place = lax.axis_index("tp")
    core = lax.axis_index("seq")
    z, x = place // 2, place % 2
    shard_words = grad.shape[1] // 2

    def shifted(step, flip=0):
        return [(p, 2 * ((p // 2 + step) % ring) + (p + flip) % 2) for p in range(tp)]

    def hop(v):
        return lax.ppermute(v, "tp", shifted(1))

    def across(v):
        return lax.ppermute(v, "tp", shifted(0, 1))

    order = jnp.stack(
        [2 * ((z - k) % ring) + x for k in range(ring)] + [2 * ((z - k) % ring) + 1 - x for k in range(ring)]
    ).astype(jnp.int32)

    own = scale_call(grad, scale)
    line1 = hop(own)
    cross0 = across(own)
    hidden = hidden_call(gate, up)
    m_a = moments_call(order, hidden, words, 0, 4, shard_words)
    line1, cross0, hidden, m_a = lax.optimization_barrier((line1, cross0, hidden, m_a))
    line2 = hop(line1)
    cross1 = across(line1)
    m_b = moments_call(order, hidden, words, 4, 4, shard_words)
    line2, cross1, m_b = lax.optimization_barrier((line2, cross1, m_b))
    line3 = hop(line2)
    cross2 = across(line2)
    total, sums_a = back_call(
        order, [own, line1, cross0, cross1], [0, 1, 4, 5], [(m_a, 0), (m_a, 1), (m_b, 0), (m_b, 1)], words
    )
    line3, cross2, total, sums_a = lax.optimization_barrier((line3, cross2, total, sums_a))
    cross3 = across(line3)
    total, sums_b = back_call(
        order, [line2, line3, cross2], [2, 3, 6], [(m_a, 2), (m_a, 3), (m_b, 2)], words, total
    )

    mine = jnp.concatenate([sums_a, sums_b], axis=0)
    both = mine + lax.ppermute(mine, "seq", [(0, 1), (1, 0)])
    other = across(jnp.stack([both[2], both[3], both[6]]))
    lines = [both[0] + other[0], both[1] + other[1], both[4] + other[2], both[5]]
    channel = lines[0]
    for k in range(1, ring):
        channel = channel + lax.ppermute(lines[k], "tp", shifted(-k))

    late = sums_call(cross3, m_b, 3)
    pairs = shifted(-3, 1)
    for flip in (0, 1):
        channel = channel + lax.ppermute(
            late, ("tp", "seq"), [(2 * a + c, 2 * b + (c + flip) % 2) for a, b in pairs for c in (0, 1)]
        )
    grad_gate, grad_up = tail_call(order, cross3, 7, words, total, gate, up)
    half = shard_words // 2
    kept = lax.dynamic_slice_in_dim(channel, core * half, half, axis=1)
    return grad_gate, grad_up, kept.T.reshape(-1)


def unpack(words):
    shifts = 4 * jnp.arange(2, dtype=jnp.int32)
    codes = jnp.bitwise_and(jnp.right_shift(words[:, :, None], shifts[None, None, :]), 15)
    return (codes.reshape(words.shape[0], words.shape[1] * 2) - 8).astype(BF16)


def by_gather(gate, up, words, scale, grad):
    g = gate.astype(F32)
    u = up.astype(F32)
    s = jax.nn.sigmoid(g)
    hidden = (g * s * u).astype(BF16)
    centered = unpack(words)
    local = (grad.astype(F32) * scale[None, :]).astype(BF16)
    whole = lax.all_gather(local, "tp", axis=1, tiled=True)
    grad_hidden = lax.dot_general(whole, centered, (((1,), (1,)), ((), ())), preferred_element_type=F32)
    moments = jnp.dot(hidden, centered, preferred_element_type=F32)
    sums = jnp.sum(whole.astype(F32) * moments, axis=0)
    grad_gate = (grad_hidden * u * s * (1.0 + g * (1.0 - s))).astype(BF16)
    grad_up = (grad_hidden * g * s).astype(BF16)
    return grad_gate, grad_up, lax.psum_scatter(sums, ("tp", "seq"), scatter_dimension=0, tiled=True)


def solution(mesh):
    tp = mesh.shape["tp"]
    per_device = functools.partial(by_ring, tp // 2) if tp == 8 and mesh.shape["seq"] == 2 else by_gather
    rows = P(("rep", "seq"), "tp")
    return jax.shard_map(
        per_device,
        mesh=mesh,
        in_specs=(rows, rows, P("tp", None), P("tp"), rows),
        out_specs=(rows, rows, P(("rep", "tp", "seq"))),
        check_vma=False,
    )
```

time: 541 us -> 136 us (0.25); the launches traced: 534 us -> 135 us
  local copies, waits for them, and re-layouts: 357 us -> 18.1 us
  matrix products: 97.9 us -> 0 us
  Pallas kernels: 0 us -> 92.3 us
  blocking collectives: 62.7 us -> 0 us
  starting transfers between devices: 0.04 us -> 17.8 us
  between operations: 14.7 us -> 0.78 us
    shift_right_arithmetic x5 -> x0, local copies, waits for them, and re-layouts: 301 us -> none  [unpack(): jnp.right_shift(words[:, :, None], shifts[None, None, :])]
    dot_general x2 -> x0, matrix products: 97.9 us -> none  [the longest x1 54.5 us: per_device(): lax.dot_general(hidden, whole_grad, (((0,), (0,)), ((), ())), preferred_e...]
    pallas_call x0 -> x8, Pallas kernels: none -> 92.3 us  [the longest x2 36.3 us: moments_call(): pl.pallas_call(moments_kernel, grid_spec=pltpu.PrefetchScalarGridSpec(num...]
    unnamed x1 -> x0, blocking collectives: 62.7 us -> none
    unnamed x7 -> x25, local copies, waits for them, and re-layouts: 56.1 us -> 15.8 us
    ppermute x0 -> x14, starting transfers between devices: none -> 17.8 us  [the longest x5 7.24 us: across(): return lax.ppermute(v, 'tp', shifted(0, 1))]
  transfers between devices with their start and end apart: 1 -> 14, of which waited for: 0 -> 2; matrix products, arithmetic and copies ran while one was open for 67% -> 3% of each run, Pallas kernels for 0% -> 66%
where the time goes in v1:
time: 136 us; the launch traced here: 135 us
  Pallas kernels  92.3 us (68%)
  local copies, waits for them, and re-layouts  18.1 us (13%)
  starting transfers between devices  17.8 us (13%)
  waiting for transfers between devices  3.54 us (3%)
  other arithmetic  2.69 us (2%)
    pallas_call x2, Pallas kernels, moments_call(): pl.pallas_call(moments_kernel, grid_spec=pltpu.PrefetchScalarGridSpec(num...  36.3 us
    pallas_call x2, Pallas kernels, back_call(): pl.pallas_call(functools.partial(back_kernel, n, first), grid_spec=pltpu....  33.5 us
    unnamed x25, local copies, waits for them, and re-layouts  15.8 us
    pallas_call x1, Pallas kernels, tail_call(): pl.pallas_call(tail_kernel, grid_spec=pltpu.PrefetchScalarGridSpec(num_sc...  10.8 us
    ppermute x5, starting transfers between devices, across(): return lax.ppermute(v, 'tp', shifted(0, 1))  7.24 us
    pallas_call x1, Pallas kernels, hidden_call(): pl.pallas_call(hidden_kernel, grid=(units // 512,), in_specs=[spec, spec]...  6.81 us
    ppermute x3, starting transfers between devices, hop(): return lax.ppermute(v, 'tp', shifted(1))  4.73 us
    ppermute x3, starting transfers between devices, by_ring(): channel = channel + lax.ppermute(lines[k], 'tp', shifted(-k))  3.27 us
  transfers between devices with their start and end apart: 14, of which 2 were waited for; matrix products, arithmetic and copies ran while one was open for 3% of the time, Pallas kernels for 66%

profile of v1, /device:TPU:0, one launch (start us, length us, event | category | flops | bytes accessed | tf_op | source)
XLA Modules:
  0.0 135.3 jit_solution(7349833769435821730)
XLA Ops:
  0.6 2.4 %scale.1.refs_0_ = bf16[384,1024]{1,0:T(8,128)(2,1)} custom-call(bf16[384,1024]{1,0:T(8,128)(2,1)} %grad_ref.1, f32[1,1024]{1,0:T(1,128)} %bitcast.21), custom_call_target="tpu_custom_call" | custom-call | flops 201326592 | bytes 1572864 | tf_op jit(solution)/shard_map/scale/pallas_call | solution.py:45
  3.0 2.9 %collective-permute-start.1 = (bf16[384,1024]{1,0:T(8,128)(2,1)}, bf16[384,1024]{1,0:T(8,128)(2,1)S(1)}, u32[]{:S(2)}, u32[]{:S(2)}) collective-permute-start(bf16[384,1024]{1,0:T(8,128)(2,1)} %scale.1.refs_0_), channel_id=1, source_target_pairs={{0,2},{2,0},{4,6},{6,4},{8,10},{10,8},{12,14},{14,12},{1,3},{3,1},... | collective-permute-start | bytes 2359304 | tf_op jit(solution)/shard_map/ppermute | solution.py:269
  6.0 1.6 %collective-permute-start = (bf16[384,1024]{1,0:T(8,128)(2,1)}, bf16[384,1024]{1,0:T(8,128)(2,1)S(1)}, u32[]{:S(2)}, u32[]{:S(2)}) collective-permute-start(bf16[384,1024]{1,0:T(8,128)(2,1)} %scale.1.refs_0_), channel_id=1, source_target_pairs={{0,4},{2,6},{4,8},{6,10},{8,12},{10,14},{12,0},{14,2},{1,5},{3,7},... | collective-permute-start | bytes 2359304 | tf_op jit(solution)/shard_map/ppermute | solution.py:266
  7.5 6.8 %hidden.1.hidden_ref = bf16[384,3584]{1,0:T(8,128)(2,1)} custom-call(bf16[384,3584]{1,0:T(8,128)(2,1)} %gate_ref.3, bf16[384,3584]{1,0:T(8,128)(2,1)} %up_ref.3), custom_call_target="tpu_custom_call" | custom-call | flops 22020096 | bytes 8257536 | tf_op jit(solution)/shard_map/hidden/pallas_call | solution.py:61
  14.4 0.1 stack.39.order_ref
  14.4 1.8 %copy-done.2 = bf16[384,3584]{1,0:T(8,128)(2,1)S(1)} copy-done((bf16[384,3584]{1,0:T(8,128)(2,1)S(1)}, bf16[384,3584]{1,0:T(8,128)(2,1)}, u32[]{:S(2)}) %copy-start.2) | copy-done | bytes 2752536
  16.2 18.0 %moments.2.refs_8_.refs_9_.refs_6_.refs_7_ = f32[4,2,384,512]{3,2,1,0:T(8,128)S(1)} custom-call(s32[8]{0:T(128)S(1)} %stack.39.order_ref, bf16[384,3584]{1,0:T(8,128)(2,1)S(1)} %copy-done.2, s32[3584,4096]{1,0:T(8,128)} %words_ref.5), custom_call_target="tpu_custom_call" | custom-call | flops 11274289152 | bytes 29360128 | tf_op jit(solution)/shard_map/moments/pallas_call | solution.py:96
  34.3 2.6 %copy-done = f32[4,2,384,512]{3,2,1,0:T(8,128)} copy-done((f32[4,2,384,512]{3,2,1,0:T(8,128)}, f32[4,2,384,512]{3,2,1,0:T(8,128)S(1)}, u32[]{:S(2)}) %copy-start) | copy-done | bytes 6291480
  36.9 0.0 collective-permute-done.1.refs_2_
  36.9 0.6 collective-permute-start.3
  37.5 1.6 %collective-permute-start.2 = (bf16[384,1024]{1,0:T(8,128)(2,1)S(1)}, bf16[384,1024]{1,0:T(8,128)(2,1)S(1)}, u32[]{:S(2)}, u32[]{:S(2)}) collective-permute-start(bf16[384,1024]{1,0:T(8,128)(2,1)S(1)} %collective-permute-done.refs_1_), channel_id=1, source_target_pairs={{0,4},{2,6},{4,8},{6,10},{8,12},{10,14},{12,0},{14,2},{1,5},{3,7},... | collective-permute-start | bytes 2359304 | tf_op jit(solution)/shard_map/ppermute | solution.py:266
  39.1 18.3 %moments.3.refs_10_.refs_11_.refs_8_.moments_ref = f32[4,2,384,512]{3,2,1,0:T(8,128)S(1)} custom-call(s32[8]{0:T(128)S(1)} %stack.39.order_ref, bf16[384,3584]{1,0:T(8,128)(2,1)S(1)} %copy-done.2, s32[3584,4096]{1,0:T(8,128)} %words_ref.5), custom_call_target="tpu_custom_call" | custom-call | flops 11274289152 | bytes 29360128 | tf_op jit(solution)/shard_map/moments/pallas_call | solution.py:96
  57.4 2.6 %copy-done.1 = f32[4,2,384,512]{3,2,1,0:T(8,128)} copy-done((f32[4,2,384,512]{3,2,1,0:T(8,128)}, f32[4,2,384,512]{3,2,1,0:T(8,128)S(1)}, u32[]{:S(2)}) %copy-start.1) | copy-done | bytes 6291480
  60.0 0.0 collective-permute-done.3.refs_3_
  60.0 0.0 collective-permute-done.2.refs_0_
  60.0 1.6 %collective-permute-start.5 = (bf16[384,1024]{1,0:T(8,128)(2,1)S(1)}, bf16[384,1024]{1,0:T(8,128)(2,1)S(1)}, u32[]{:S(2)}, u32[]{:S(2)}) collective-permute-start(bf16[384,1024]{1,0:T(8,128)(2,1)S(1)} %collective-permute-done.2.refs_0_), channel_id=1, source_target_pairs={{0,2},{2,0},{4,6},{6,4},{8,10},{10,8},{12,14},{14,12},{1,3},{3,1},... | collective-permute-start | bytes 2359304 | tf_op jit(solution)/shard_map/ppermute | solution.py:269
  61.6 1.6 %collective-permute-start.4 = (bf16[384,1024]{1,0:T(8,128)(2,1)S(1)}, bf16[384,1024]{1,0:T(8,128)(2,1)}, u32[]{:S(2)}, u32[]{:S(2)}) collective-permute-start(bf16[384,1024]{1,0:T(8,128)(2,1)S(1)} %collective-permute-done.2.refs_0_), channel_id=1, source_target_pairs={{0,4},{2,6},{4,8},{6,10},{8,12},{10,14},{12,0},{14,2},{1,5},{3,7},... | collective-permute-start | bytes 2359304 | tf_op jit(solution)/shard_map/ppermute | solution.py:266
  63.2 18.4 %back.2 = (f32[384,3584]{1,0:T(8,128)S(1)}, f32[4,2,512]{2,1,0:T(2,128)S(1)}) custom-call(s32[8]{0:T(128)S(1)} %stack.39.order_ref, bf16[384,1024]{1,0:T(8,128)(2,1)S(1)} %copy-done.9, bf16[384,1024]{1,0:T(8,128)(2,1)S(1)} %collective-permute-done.refs_1_, bf16[384,1024]{1,0:T(8,128)(2,1)S(1)} %collective-permute-done.1.refs_2_, ...), custom_call_target="tpu_custom_call" | custom-call | flops 11274289152 | bytes 29360128 | tf_op jit(solution)/shard_map/back/pallas_call | solution.py:173
  81.5 0.0 collective-permute-done.5.refs_2_
  81.6 0.6 collective-permute-start.6
  82.2 15.1 %back.3 = (f32[384,3584]{1,0:T(8,128)S(1)}, f32[3,2,512]{2,1,0:T(2,128)S(1)}) custom-call(s32[8]{0:T(128)S(1)} %stack.39.order_ref, bf16[384,1024]{1,0:T(8,128)(2,1)S(1)} %collective-permute-done.2.refs_0_, bf16[384,1024]{1,0:T(8,128)(2,1)} %collective-permute-done.4.refs_1_, ...), custom_call_target="tpu_custom_call", output_to_operand_aliasing={{0}: (10, {})} | custom-call | flops 8455716864 | bytes 22020096 | tf_op jit(solution)/shard_map/back/pallas_call | solution.py:173
  97.3 2.4 %copy-done.3 = f32[384,3584]{1,0:T(8,128)} copy-done((f32[384,3584]{1,0:T(8,128)}, f32[384,3584]{1,0:T(8,128)S(1)}, u32[]{:S(2)}) %copy-start.3) | copy-done | bytes 5505048
  99.7 0.1 collective-permute-start.7
  99.8 1.2 collective-permute-done.7
  101.0 0.6 add.100
  101.6 0.7 slice.40
  102.3 0.7 slice.39
  103.0 1.5 %collective-permute-start.8 = (f32[3,2,512]{2,1,0:T(2,128)S(1)}, f32[3,2,512]{2,1,0:T(2,128)}, u32[]{:S(2)}, u32[]{:S(2)}) collective-permute-start(f32[3,2,512]{2,1,0:T(2,128)S(1)} %pad_maximum_fusion), channel_id=1, source_target_pairs={{0,2},{2,0},{4,6},{6,4},{8,10},{10,8},{12,14},{14,12},{1,3},{3,1},... | collective-permute-start | bytes 36872 | tf_op jit(solution)/shard_map/ppermute | solution.py:269
  104.6 2.3 %collective-permute-done.8 = f32[3,2,512]{2,1,0:T(2,128)} collective-permute-done((f32[3,2,512]{2,1,0:T(2,128)S(1)}, f32[3,2,512]{2,1,0:T(2,128)}, u32[]{:S(2)}, u32[]{:S(2)}) %collective-permute-start.8) | collective-permute-done | bytes 12320 | tf_op jit(solution)/shard_map/ppermute | solution.py:269
  106.9 1.3 fusion.2
  108.2 1.2 collective-permute-start.10
  109.5 1.1 collective-permute-start.9
  110.6 0.9 collective-permute-start.11
  111.5 0.9 copy-done.7
  112.4 2.4 %sums.1 = f32[2,512]{1,0:T(2,128)} custom-call(bf16[384,1024]{1,0:T(8,128)(2,1)} %copy-done.7, f32[4,2,384,512]{3,2,1,0:T(8,128)} %copy-done.1), custom_call_target="tpu_custom_call" | custom-call | flops 786432 | bytes 2359296 | tf_op jit(solution)/shard_map/sums/pallas_call | solution.py:205
  114.8 0.3 collective-permute-start.13
  115.1 2.3 %collective-permute-start.12 = (f32[2,512]{1,0:T(2,128)}, f32[2,512]{1,0:T(2,128)S(1)}, u32[]{:S(2)}, u32[]{:S(2)}) collective-permute-start(f32[2,512]{1,0:T(2,128)} %sums.1), channel_id=1, source_target_pairs={{0,6},{1,7},{2,4},{3,5},{4,10},{5,11},{6,8},{7,9},{8,14},{9,15},{1... | collective-permute-start | bytes 12296 | tf_op jit(solution)/shard_map/ppermute | solution.py:307
  117.4 2.6 %copy-done.4 = f32[384,3584]{1,0:T(8,128)S(1)} copy-done((f32[384,3584]{1,0:T(8,128)S(1)}, f32[384,3584]{1,0:T(8,128)}, u32[]{:S(2)}) %copy-start.4) | copy-done | bytes 5505048
  119.9 1.8 %copy-done.6 = bf16[384,3584]{1,0:T(8,128)(2,1)S(1)} copy-done((bf16[384,3584]{1,0:T(8,128)(2,1)S(1)}, bf16[384,3584]{1,0:T(8,128)(2,1)}, u32[]{:S(2)}) %copy-start.6) | copy-done | bytes 2752536
  121.7 1.1 copy-done.8
  122.8 10.8 %tail.1 = (bf16[384,3584]{1,0:T(8,128)(2,1)}, bf16[384,3584]{1,0:T(8,128)(2,1)}) custom-call(s32[8]{0:T(128)S(1)} %stack.39.order_ref, bf16[384,1024]{1,0:T(8,128)(2,1)S(1)} %copy-done.8, s32[3584,4096]{1,0:T(8,128)} %words_ref.5, f32[384,3584]{1,0:T(8,128)S(1)} %copy-done.4, bf16[384,3584]{1,0:T(8,128)(2,1)S(1)} %copy-done.5, bf16[384,3584]{1,0:T(8,128)(2,1)S(1)} %copy-done.6), custom_call_target="tpu_custom_call" | custom-call | flops 2818572288 | bytes 23855104 | tf_op jit(solution)/shard_map/tail/pallas_call | solution.py:234
  133.6 0.0 collective-permute-done.10
  133.6 0.0 collective-permute-done.9
  133.7 0.0 collective-permute-done.13
  133.7 0.0 collective-permute-done.12
  133.7 0.7 fusion.3
  134.4 0.1 copy.9
  134.5 0.7 reshape.16
  (24 shorter events, 0.1 us)
Async XLA Ops:
  3.0 33.8 %collective-permute-start.1 = (bf16[384,1024]{1,0:T(8,128)(2,1)}, bf16[384,1024]{1,0:T(8,128)(2,1)S(1)}, u32[]{:S(2)}, u32[]{:S(2)}) collective-permute-start(bf16[384,1024]{1,0:T(8,128)(2,1)} %scale.1.refs_0_), channel_id=1, source_target_pairs={{0,2},{2,0},{4,6},{6,4},{8,10},{10,8},{12,14},{14,12},{1,3},{3,1},... | collective-permute-start | bytes 2359304 | tf_op jit(solution)/shard_map/ppermute | solution.py:269
  6.0 30.9 %collective-permute-start = (bf16[384,1024]{1,0:T(8,128)(2,1)}, bf16[384,1024]{1,0:T(8,128)(2,1)S(1)}, u32[]{:S(2)}, u32[]{:S(2)}) collective-permute-start(bf16[384,1024]{1,0:T(8,128)(2,1)} %scale.1.refs_0_), channel_id=1, source_target_pairs={{0,4},{2,6},{4,8},{6,10},{8,12},{10,14},{12,0},{14,2},{1,5},{3,7},... | collective-permute-start | bytes 2359304 | tf_op jit(solution)/shard_map/ppermute | solution.py:266
  14.4 1.8 %copy-start.2 = (bf16[384,3584]{1,0:T(8,128)(2,1)S(1)}, bf16[384,3584]{1,0:T(8,128)(2,1)}, u32[]{:S(2)}) copy-start(bf16[384,3584]{1,0:T(8,128)(2,1)} %hidden.1.hidden_ref) | copy-start | bytes 8257540
  34.3 2.6 %copy-start = (f32[4,2,384,512]{3,2,1,0:T(8,128)}, f32[4,2,384,512]{3,2,1,0:T(8,128)S(1)}, u32[]{:S(2)}) copy-start(f32[4,2,384,512]{3,2,1,0:T(8,128)S(1)} %moments.2.refs_8_.refs_9_.refs_6_.refs_7_) | copy-start | bytes 18874372
  36.9 26.3 %copy-start.9 = (bf16[384,1024]{1,0:T(8,128)(2,1)S(1)}, bf16[384,1024]{1,0:T(8,128)(2,1)}, u32[]{:S(2)}) copy-start(bf16[384,1024]{1,0:T(8,128)(2,1)} %scale.1.refs_0_) | copy-start | bytes 2359300
  36.9 23.1 %collective-permute-start.3 = (bf16[384,1024]{1,0:T(8,128)(2,1)S(1)}, bf16[384,1024]{1,0:T(8,128)(2,1)S(1)}, u32[]{:S(2)}, u32[]{:S(2)}) collective-permute-start(bf16[384,1024]{1,0:T(8,128)(2,1)S(1)} %collective-permute-done.refs_1_), channel_id=1, source_target_pairs={{0,2},{2,0},{4,6},{6,4},{8,10},{10,8},{12,14},{14,12},{1,3},{3,1},... | collective-permute-start | bytes 2359304 | tf_op jit(solution)/shard_map/ppermute | solution.py:269
  37.5 22.5 %collective-permute-start.2 = (bf16[384,1024]{1,0:T(8,128)(2,1)S(1)}, bf16[384,1024]{1,0:T(8,128)(2,1)S(1)}, u32[]{:S(2)}, u32[]{:S(2)}) collective-permute-start(bf16[384,1024]{1,0:T(8,128)(2,1)S(1)} %collective-permute-done.refs_1_), channel_id=1, source_target_pairs={{0,4},{2,6},{4,8},{6,10},{8,12},{10,14},{12,0},{14,2},{1,5},{3,7},... | collective-permute-start | bytes 2359304 | tf_op jit(solution)/shard_map/ppermute | solution.py:266
  39.1 43.1 %slice-start = ((s8[6291456]{0:T(1024)(128)(4,1)}), s8[4194304]{0:T(1024)(128)(4,1)S(1)}, s32[]{:S(2)}) async-start(s8[6291456]{0:T(1024)(128)(4,1)} %bitcast.19), calls=%async_computation | async-start | bytes 8388608
  57.4 2.6 %copy-start.1 = (f32[4,2,384,512]{3,2,1,0:T(8,128)}, f32[4,2,384,512]{3,2,1,0:T(8,128)S(1)}, u32[]{:S(2)}) copy-start(f32[4,2,384,512]{3,2,1,0:T(8,128)S(1)} %moments.3.refs_10_.refs_11_.refs_8_.moments_ref) | copy-start | bytes 18874372
  60.0 22.2 %slice-start.1 = ((s8[6291456]{0:T(1024)(128)(4,1)}), s8[2097152]{0:T(1024)(128)(4,1)S(1)}, s32[]{:S(2)}) async-start(s8[6291456]{0:T(1024)(128)(4,1)} %bitcast.19), calls=%async_computation.1 | async-start | bytes 4194304
  60.0 21.5 %collective-permute-start.5 = (bf16[384,1024]{1,0:T(8,128)(2,1)S(1)}, bf16[384,1024]{1,0:T(8,128)(2,1)S(1)}, u32[]{:S(2)}, u32[]{:S(2)}) collective-permute-start(bf16[384,1024]{1,0:T(8,128)(2,1)S(1)} %collective-permute-done.2.refs_0_), channel_id=1, source_target_pairs={{0,2},{2,0},{4,6},{6,4},{8,10},{10,8},{12,14},{14,12},{1,3},{3,1},... | collective-permute-start | bytes 2359304 | tf_op jit(solution)/shard_map/ppermute | solution.py:269
  61.6 20.0 %collective-permute-start.4 = (bf16[384,1024]{1,0:T(8,128)(2,1)S(1)}, bf16[384,1024]{1,0:T(8,128)(2,1)}, u32[]{:S(2)}, u32[]{:S(2)}) collective-permute-start(bf16[384,1024]{1,0:T(8,128)(2,1)S(1)} %collective-permute-done.2.refs_0_), channel_id=1, source_target_pairs={{0,4},{2,6},{4,8},{6,10},{8,12},{10,14},{12,0},{14,2},{1,5},{3,7},... | collective-permute-start | bytes 2359304 | tf_op jit(solution)/shard_map/ppermute | solution.py:266
  81.6 29.9 %collective-permute-start.6 = (bf16[384,1024]{1,0:T(8,128)(2,1)}, bf16[384,1024]{1,0:T(8,128)(2,1)S(1)}, u32[]{:S(2)}, u32[]{:S(2)}) collective-permute-start(bf16[384,1024]{1,0:T(8,128)(2,1)} %collective-permute-done.4.refs_1_), channel_id=1, source_target_pairs={{0,2},{2,0},{4,6},{6,4},{8,10},{10,8},{12,14},{14,12},{1,3},{3,1},... | collective-permute-start | bytes 2359304 | tf_op jit(solution)/shard_map/ppermute | solution.py:269
  97.3 2.4 %copy-start.3 = (f32[384,3584]{1,0:T(8,128)}, f32[384,3584]{1,0:T(8,128)S(1)}, u32[]{:S(2)}) copy-start(f32[384,3584]{1,0:T(8,128)S(1)} %get-tuple-element.32.total_ref) | copy-start | bytes 16515076
  99.7 17.6 %copy-start.5 = (bf16[384,3584]{1,0:T(8,128)(2,1)S(1)}, bf16[384,3584]{1,0:T(8,128)(2,1)}, u32[]{:S(2)}) copy-start(bf16[384,3584]{1,0:T(8,128)(2,1)} %gate_ref.3) | copy-start | bytes 8257540
  99.7 1.3 collective-permute-start.7
  103.0 3.9 %collective-permute-start.8 = (f32[3,2,512]{2,1,0:T(2,128)S(1)}, f32[3,2,512]{2,1,0:T(2,128)}, u32[]{:S(2)}, u32[]{:S(2)}) collective-permute-start(f32[3,2,512]{2,1,0:T(2,128)S(1)} %pad_maximum_fusion), channel_id=1, source_target_pairs={{0,2},{2,0},{4,6},{6,4},{8,10},{10,8},{12,14},{14,12},{1,3},{3,1},... | collective-permute-start | bytes 36872 | tf_op jit(solution)/shard_map/ppermute | solution.py:269
  108.2 25.4 %collective-permute-start.10 = (f32[2,512]{1,0:T(2,128)}, f32[2,512]{1,0:T(2,128)}, u32[]{:S(2)}, u32[]{:S(2)}) collective-permute-start(f32[2,512]{1,0:T(2,128)} %get-tuple-element.38), channel_id=1, source_target_pairs={{0,8},{2,10},{4,12},{6,14},{8,0},{10,2},{12,4},{14,6},{1,9},{3,11}... | collective-permute-start | bytes 12296 | tf_op jit(solution)/shard_map/ppermute | solution.py:302
  109.5 24.2 %collective-permute-start.9 = (f32[2,512]{1,0:T(2,128)S(1)}, f32[2,512]{1,0:T(2,128)}, u32[]{:S(2)}, u32[]{:S(2)}) collective-permute-start(f32[2,512]{1,0:T(2,128)S(1)} %get-tuple-element.39), channel_id=1, source_target_pairs={{0,12},{2,14},{4,0},{6,2},{8,4},{10,6},{12,8},{14,10},{1,13},{3,15... | collective-permute-start | bytes 12296 | tf_op jit(solution)/shard_map/ppermute | solution.py:302
  110.6 23.1 %collective-permute-start.11 = (f32[2,512]{1,0:T(2,128)S(1)}, f32[2,512]{1,0:T(2,128)}, u32[]{:S(2)}, u32[]{:S(2)}) collective-permute-start(f32[2,512]{1,0:T(2,128)S(1)} %get-tuple-element.40), channel_id=1, source_target_pairs={{0,4},{2,6},{4,8},{6,10},{8,12},{10,14},{12,0},{14,2},{1,5},{3,7},... | collective-permute-start | bytes 12296 | tf_op jit(solution)/shard_map/ppermute | solution.py:302
  111.5 0.9 copy-start.7
  114.8 18.8 %collective-permute-start.13 = (f32[2,512]{1,0:T(2,128)}, f32[2,512]{1,0:T(2,128)S(1)}, u32[]{:S(2)}, u32[]{:S(2)}) collective-permute-start(f32[2,512]{1,0:T(2,128)} %sums.1), channel_id=1, source_target_pairs={{0,7},{1,6},{2,5},{3,4},{4,11},{5,10},{6,9},{7,8},{8,15},{9,14},{1... | collective-permute-start | bytes 12296 | tf_op jit(solution)/shard_map/ppermute | solution.py:307
  115.1 18.6 %collective-permute-start.12 = (f32[2,512]{1,0:T(2,128)}, f32[2,512]{1,0:T(2,128)S(1)}, u32[]{:S(2)}, u32[]{:S(2)}) collective-permute-start(f32[2,512]{1,0:T(2,128)} %sums.1), channel_id=1, source_target_pairs={{0,6},{1,7},{2,4},{3,5},{4,10},{5,11},{6,8},{7,9},{8,14},{9,15},{1... | collective-permute-start | bytes 12296 | tf_op jit(solution)/shard_map/ppermute | solution.py:307
  117.4 2.6 %copy-start.4 = (f32[384,3584]{1,0:T(8,128)S(1)}, f32[384,3584]{1,0:T(8,128)}, u32[]{:S(2)}) copy-start(f32[384,3584]{1,0:T(8,128)} %copy-done.3) | copy-start | bytes 16515076
  119.9 1.8 %copy-start.6 = (bf16[384,3584]{1,0:T(8,128)(2,1)S(1)}, bf16[384,3584]{1,0:T(8,128)(2,1)}, u32[]{:S(2)}) copy-start(bf16[384,3584]{1,0:T(8,128)(2,1)} %up_ref.3) | copy-start | bytes 8257540
  121.7 1.1 copy-start.8

commit v2 on v0

v2 whole, which is shorter than its diff:
```python
import functools

import jax
import jax.numpy as jnp
from jax import lax
from jax.experimental import pallas as pl
from jax.experimental.pallas import tpu as pltpu
from jax.sharding import PartitionSpec as P

F32 = jnp.float32
BF16 = jnp.bfloat16
VMEM_LIMIT = 48 << 20


def sigmoid(v):
    return 0.5 * jnp.tanh(0.5 * v) + 0.5


def nibbles(words):
    low = (jnp.bitwise_and(words, 15) - 8).astype(F32).astype(BF16)
    high = (jnp.right_shift(words, 4) - 8).astype(F32).astype(BF16)
    return jnp.concatenate([low, high], axis=1)


HELD = pl.BlockSpec(memory_space=pltpu.VMEM)


def cost(flops, bytes_accessed):
    return pl.CostEstimate(flops=int(flops), bytes_accessed=int(bytes_accessed), transcendentals=0)


def scale_kernel(grad_ref, scale_ref, out_ref):
    width = grad_ref.shape[1]
    half = width // 2
    scaled = (grad_ref[...].astype(F32) * scale_ref[...]).astype(BF16)
    source = lax.broadcasted_iota(jnp.int32, (256, 256), 0)
    target = lax.broadcasted_iota(jnp.int32, (256, 256), 1)
    wanted = jnp.where(target < 128, 2 * target, 2 * target - 255)
    pick = (source == wanted).astype(F32).astype(BF16)
    for b in range(width // 256):
        sorted_block = jnp.dot(scaled[:, 256 * b:256 * b + 256], pick, preferred_element_type=F32).astype(BF16)
        out_ref[:, 128 * b:128 * b + 128] = sorted_block[:, :128]
        out_ref[:, half + 128 * b:half + 128 * b + 128] = sorted_block[:, 128:]


def scale_call(grad, scale):
    rows, width = grad.shape
    return pl.pallas_call(
        scale_kernel,
        out_shape=jax.ShapeDtypeStruct((rows, width), BF16),
        name="scale",
        cost_estimate=cost(2 * rows * width * 256, 4 * rows * width),
    )(grad, scale.reshape(1, width))


def hidden_kernel(gate_ref, up_ref, out_ref):
    g = gate_ref[...].astype(F32)
    out_ref[...] = (g * sigmoid(g) * up_ref[...].astype(F32)).astype(BF16)


def hidden_call(gate, up):
    rows, units = gate.shape
    spec = pl.BlockSpec((96, units), lambda i: (i, 0))
    return pl.pallas_call(
        hidden_kernel,
        grid=(rows // 96,),
        in_specs=[spec, spec],
        out_specs=spec,
        out_shape=jax.ShapeDtypeStruct((rows, units), BF16),
        name="hidden",
        compiler_params=pltpu.CompilerParams(vmem_limit_bytes=VMEM_LIMIT),
        cost_estimate=cost(16 * rows * units, 6 * rows * units),
    )(gate, up)


def moments_kernel(n_known, order_ref, hidden_ref, words_ref, *refs):
    grads, out_ref, sums = refs[:n_known], refs[n_known], refs[n_known + 1:]
    total = None
    for k in range(0, hidden_ref.shape[1], BLOCK):
        product = jnp.dot(
            hidden_ref[:, k:k + BLOCK], nibbles(words_ref[k:k + BLOCK, :]), preferred_element_type=F32
        )
        total = product if total is None else total + product
    out_ref[0] = total
    for s in range(n_known):

        @pl.when(pl.program_id(0) == s)
        def _(s=s):
            sums[s][...] = jnp.sum(grads[s][...].astype(F32) * out_ref[0], axis=0, keepdims=True)


def moments_call(order, shards, hidden, words, shard_words, grads):
    rows, units = hidden.shape
    n = len(shards)
    first, second = shards[0], shards[n // 2]

    def place(s, o):
        return 0, o[jnp.where(s < n // 2, first + s, second - n // 2 + s)]

    width = 2 * shard_words
    out = pl.pallas_call(
        functools.partial(moments_kernel, len(grads)),
        grid_spec=pltpu.PrefetchScalarGridSpec(
            num_scalar_prefetch=1,
            grid=(n,),
            in_specs=[
                HELD,
                pl.BlockSpec((units, shard_words), place),
            ]
            + [HELD] * len(grads),
            out_specs=[pl.BlockSpec((1, rows, width), lambda s, o: (s, 0, 0))]
            + [pl.BlockSpec((1, width), lambda s, o: (0, 0))] * len(grads),
        ),
        out_shape=[jax.ShapeDtypeStruct((n, rows, width), F32)]
        + [jax.ShapeDtypeStruct((1, width), F32)] * len(grads),
        name="moments",
        compiler_params=pltpu.CompilerParams(vmem_limit_bytes=VMEM_LIMIT),
        cost_estimate=cost(4 * n * rows * units * shard_words, 4 * n * units * shard_words),
    )(order, hidden, words, *grads)
    return out[0], out[1:]


BLOCK = 512
SUM_ROWS = 64


def sums_kernel(core_ref, *refs):
    grads, moments, known, outs = refs[:2], refs[2:4], refs[4:10], refs[10:]
    late = [
        jnp.sum(g[...].astype(F32) * m[0], axis=0, keepdims=True) for g, m in zip(grads, moments)
    ]
    rows = [ref[...] for ref in known] + late
    quarter = rows[0].shape[1] // 4
    first = core_ref[0] == 0
    for place, row in enumerate(rows):
        low = jnp.concatenate([row[:, :quarter], row[:, 2 * quarter:3 * quarter]], axis=1)
        high = jnp.concatenate([row[:, quarter:2 * quarter], row[:, 3 * quarter:]], axis=1)
        crossed, k = divmod(place, 4)
        outs[2 * crossed][k:k + 1, :] = jnp.where(first, low, high)
        outs[2 * crossed + 1][k:k + 1, :] = jnp.where(first, high, low)


def sums_call(core, moments, places, grads, known):
    rows, width = grads[0].shape
    n = len(places)
    return pl.pallas_call(
        sums_kernel,
        grid_spec=pltpu.PrefetchScalarGridSpec(
            num_scalar_prefetch=1,
            grid=(1,),
            in_specs=[HELD] * n
            + [pl.BlockSpec((1, rows, width), functools.partial(lambda s, i, c: (s, 0, 0), s)) for s in places]
            + [HELD] * len(known),
            out_specs=[pl.BlockSpec((4, width // 2), lambda i, c: (0, 0))] * 4,
        ),
        out_shape=[jax.ShapeDtypeStruct((4, width // 2), F32)] * 4,
        name="sums",
        compiler_params=pltpu.CompilerParams(vmem_limit_bytes=VMEM_LIMIT),
        cost_estimate=cost(2 * n * rows * width, 6 * n * rows * width),
    )(core.reshape(1).astype(jnp.int32), *grads, *([moments] * n), *known)


def product_kernel(n, n_sums, finish, order_ref, *refs):
    grads, words, moments = refs[:n], refs[n:2 * n], refs[2 * n:2 * n + n_sums]
    rest = refs[2 * n + n_sums:]
    sums = rest[len(rest) - n_sums:]
    step = pl.program_id(0)
    total = None
    for grad_ref, word_ref in zip(grads, words):
        product = lax.dot_general(
            grad_ref[...], nibbles(word_ref[...]), (((1,), (1,)), ((), ())), preferred_element_type=F32
        )
        total = product if total is None else total + product
    finish(total, *rest[:len(rest) - n_sums])
    if n_sums == 0:
        return
    rows = moments[0].shape[1]

    @pl.when(step == 0)
    def _():
        for ref in sums:
            ref[...] = jnp.zeros_like(ref)

    @pl.when(step * rows < grads[0].shape[0])
    def _():
        part = pl.ds(pl.multiple_of(step * rows, rows), rows)
        for s in range(n_sums):
            terms = grads[s][part, :].astype(F32) * moments[s][0]
            sums[s][...] += jnp.sum(terms, axis=0, keepdims=True)


def product_call(name, finish, order, words, shards, grads, moments, wide_in, wide_out):
    n = len(shards)
    units = words.shape[0]
    rows, width = grads[0].shape
    last_rows = rows // SUM_ROWS - 1
    wide = pl.BlockSpec((rows, BLOCK), lambda i, o: (0, i))
    vector = pl.BlockSpec((1, width), lambda i, o: (0, 0))
    in_specs = [HELD] * n
    for s in shards:
        in_specs.append(pl.BlockSpec((BLOCK, width // 2), functools.partial(lambda s, i, o: (i, o[s]), s)))
    for _, s in moments:
        place = functools.partial(lambda s, i, o: (s, jnp.minimum(i, last_rows), 0), s)
        in_specs.append(pl.BlockSpec((1, SUM_ROWS, width), place))
    out = pl.pallas_call(
        functools.partial(product_kernel, n, len(moments), finish),
        grid_spec=pltpu.PrefetchScalarGridSpec(
            num_scalar_prefetch=1,
            grid=(units // BLOCK,),
            in_specs=in_specs + [wide] * len(wide_in),
            out_specs=[wide] * len(wide_out) + [vector] * len(moments),
        ),
        out_shape=[jax.ShapeDtypeStruct((rows, units), kind) for kind in wide_out]
        + [jax.ShapeDtypeStruct((1, width), F32)] * len(moments),
        name=name,
        compiler_params=pltpu.CompilerParams(vmem_limit_bytes=VMEM_LIMIT),
        cost_estimate=cost(2 * n * rows * units * width, 2 * n * units * width),
    )(order, *grads, *([words] * n), *[m for m, _ in moments], *wide_in)
    return out[:len(wide_out)], out[len(wide_out):]


def back(product, total_ref):
    total_ref[...] = product


def tail(product, before_ref, gate_ref, up_ref, gate_out_ref, up_out_ref):
    grad_hidden = before_ref[...] + product
    g = gate_ref[...].astype(F32)
    s = sigmoid(g)
    gate_out_ref[...] = (grad_hidden * up_ref[...].astype(F32) * s * (1.0 + g * (1.0 - s))).astype(BF16)
    up_out_ref[...] = (grad_hidden * g * s).astype(BF16)


def by_ring(gate, up, words, scale, grad):
    ring = 4
    place = lax.axis_index("tp")
    core = lax.axis_index("seq")
    z, x = place // 2, place % 2
    shard_words = grad.shape[1] // 2
    together = lax.optimization_barrier

    def shifted(step, flip=0):
        return [(p, 2 * ((p // 2 + step) % ring) + (p + flip) % 2) for p in range(2 * ring)]

    def move(v, step, flip=0):
        return lax.ppermute(v, "tp", shifted(step, flip))

    k = jnp.arange(2 * ring, dtype=jnp.int32)
    order = 2 * ((z + ring - k % ring) % ring) + (x + k // ring) % 2

    own = scale_call(grad, scale)
    line1 = move(own, 1)
    cross0 = move(own, 0, 1)
    hidden = hidden_call(gate, up)
    own, hidden = together((own, hidden))
    line3 = move(own, -1)
    m_later, _ = moments_call(order, [2, 3, 6, 7], hidden, words, shard_words, [])
    line1, cross0, m_later, hidden = together((line1, cross0, m_later, hidden))
    line2 = move(line1, 1)
    cross1 = move(line1, 0, 1)
    m_soon, (s0, s1, c0) = moments_call(order, [0, 1, 4, 5], hidden, words, shard_words, [own, line1, cross0])
    line3, cross1, m_soon = together((line3, cross1, m_soon))
    cross2 = move(cross1, 1)
    cross3 = move(line3, 0, 1)
    (total,), (s2, s3, c1) = product_call(
        "back", back, order, words, [2, 3, 5, 0, 1, 4], [line2, line3, cross1, own, line1, cross0],
        [(m_later, 0), (m_later, 1), (m_soon, 3)], [], [F32],
    )
    lines, lines_other, crossed, crossed_other = sums_call(
        core, m_later, [2, 3], [cross2, cross3], [s0, s1, s2, s3, c0, c1]
    )
    diagonal = [(2 * a + c, 2 * b + 1 - c) for a, b in shifted(0, 1) for c in (0, 1)]
    lines = lines + lax.ppermute(lines_other, "seq", [(0, 1), (1, 0)])
    lines = lines + move(crossed, 0, 1) + lax.ppermute(crossed_other, ("tp", "seq"), diagonal)
    sent = [move(lines[k:k + 1], -k) for k in range(1, ring)]
    (grad_gate, grad_up), _ = product_call(
        "tail", tail, order, words, [6, 7], [cross2, cross3], [], [total, gate, up], [BF16, BF16]
    )
    channel = lines[0:1] + sent[0] + sent[1] + sent[2]
    return grad_gate, grad_up, channel.reshape(2, shard_words // 2).T.reshape(-1)


def unpack(words):
    shifts = 4 * jnp.arange(2, dtype=jnp.int32)
    codes = jnp.bitwise_and(jnp.right_shift(words[:, :, None], shifts[None, None, :]), 15)
    return (codes.reshape(words.shape[0], words.shape[1] * 2) - 8).astype(BF16)


def by_gather(gate, up, words, scale, grad):
    g = gate.astype(F32)
    u = up.astype(F32)
    s = jax.nn.sigmoid(g)
    hidden = (g * s * u).astype(BF16)
    centered = unpack(words)
    local = (grad.astype(F32) * scale[None, :]).astype(BF16)
    whole = lax.all_gather(local, "tp", axis=1, tiled=True)
    grad_hidden = lax.dot_general(whole, centered, (((1,), (1,)), ((), ())), preferred_element_type=F32)
    moments = jnp.dot(hidden, centered, preferred_element_type=F32)
    sums = jnp.sum(whole.astype(F32) * moments, axis=0)
    grad_gate = (grad_hidden * u * s * (1.0 + g * (1.0 - s))).astype(BF16)
    grad_up = (grad_hidden * g * s).astype(BF16)
    return grad_gate, grad_up, lax.psum_scatter(sums, ("tp", "seq"), scatter_dimension=0, tiled=True)


def solution(mesh):
    tp = mesh.shape["tp"]
    per_device = by_ring if tp == 8 and mesh.shape["seq"] == 2 else by_gather
    rows = P(("rep", "seq"), "tp")
    return jax.shard_map(
        per_device,
        mesh=mesh,
        in_specs=(rows, rows, P("tp", None), P("tp"), rows),
        out_specs=(rows, rows, P(("rep", "tp", "seq"))),
        check_vma=False,
    )
```

time: 541 us -> 118 us (0.22); the launches traced: 534 us -> 117 us
  local copies, waits for them, and re-layouts: 357 us -> 2.67 us
  matrix products: 97.9 us -> 0 us
  Pallas kernels: 0 us -> 87 us
  blocking collectives: 62.7 us -> 0 us
  starting transfers between devices: 0.04 us -> 25 us
  between operations: 14.7 us -> 0.74 us
    shift_right_arithmetic x5 -> x0, local copies, waits for them, and re-layouts: 301 us -> none  [unpack(): jnp.right_shift(words[:, :, None], shifts[None, None, :])]
    dot_general x2 -> x0, matrix products: 97.9 us -> none  [the longest x1 54.5 us: per_device(): lax.dot_general(hidden, whole_grad, (((0,), (0,)), ((), ())), preferred_e...]
    pallas_call x0 -> x7, Pallas kernels: none -> 87 us  [the longest x2 42 us: product_call(): pl.pallas_call(functools.partial(product_kernel, n, len(moments), finish)...]
    unnamed x1 -> x0, blocking collectives: 62.7 us -> none
    unnamed x7 -> x6, local copies, waits for them, and re-layouts: 56.1 us -> 1.79 us
    ppermute x0 -> x13, starting transfers between devices: none -> 25 us  [the longest x11 23.7 us: move(): return lax.ppermute(v, 'tp', shifted(step, flip))]
  transfers between devices with their start and end apart: 1 -> 13, of which waited for: 0 -> 1; matrix products, arithmetic and copies ran while one was open for 67% -> 0% of each run, Pallas kernels for 0% -> 70%
where the time goes in v2:
time: 118 us; the launch traced here: 117 us
  Pallas kernels  87 us (74%)
  starting transfers between devices  25 us (21%)
  local copies, waits for them, and re-layouts  2.67 us (2%)
  waiting for transfers between devices  1.92 us (2%)
    pallas_call x2, Pallas kernels, product_call(): pl.pallas_call(functools.partial(product_kernel, n, len(moments), finish)...  42 us
    pallas_call x2, Pallas kernels, moments_call(): pl.pallas_call(functools.partial(moments_kernel, len(grads)), grid_spec=p...  36.5 us
    ppermute x11, starting transfers between devices, move(): return lax.ppermute(v, 'tp', shifted(step, flip))  23.7 us
    pallas_call x1, Pallas kernels, hidden_call(): pl.pallas_call(hidden_kernel, grid=(rows // 96,), in_specs=[spec, spec],...  3.51 us
    pallas_call x1, Pallas kernels, sums_call(): pl.pallas_call(sums_kernel, grid_spec=pltpu.PrefetchScalarGridSpec(num_sc...  2.55 us
    pallas_call x1, Pallas kernels, scale_call(): pl.pallas_call(scale_kernel, out_shape=jax.ShapeDtypeStruct((rows, width)...  2.4 us
  transfers between devices with their start and end apart: 13, of which 1 were waited for; matrix products, arithmetic and copies ran while one was open for 0% of the time, Pallas kernels for 70%

profile of v2, /device:TPU:0, one launch (start us, length us, event | category | flops | bytes accessed | tf_op | source)
XLA Modules:
  0.0 117.4 jit_solution(11974898690442938320)
XLA Ops:
  0.6 2.4 %scale.1.refs_0_.refs_3_ = bf16[384,1024]{1,0:T(8,128)(2,1)} custom-call(bf16[384,1024]{1,0:T(8,128)(2,1)} %grad_ref.1, f32[1,1024]{1,0:T(1,128)} %bitcast.4), custom_call_target="tpu_custom_call" | custom-call | flops 201326592 | bytes 1572864 | tf_op jit(solution)/shard_map/scale/pallas_call | solution.py:48
  3.0 2.9 %collective-permute-start.2 = (bf16[384,1024]{1,0:T(8,128)(2,1)}, bf16[384,1024]{1,0:T(8,128)(2,1)}, u32[]{:S(2)}, u32[]{:S(2)}) collective-permute-start(bf16[384,1024]{1,0:T(8,128)(2,1)} %scale.1.refs_0_.refs_3_), channel_id=1, source_target_pairs={{0,2},{2,0},{4,6},{6,4},{8,10},{10,8},{12,14},{14,12},{1,3},{3,1},... | collective-permute-start | bytes 2359304 | tf_op jit(solution)/shard_map/ppermute | solution.py:246
  6.0 1.6 %collective-permute-start.1 = (bf16[384,1024]{1,0:T(8,128)(2,1)}, bf16[384,1024]{1,0:T(8,128)(2,1)}, u32[]{:S(2)}, u32[]{:S(2)}) collective-permute-start(bf16[384,1024]{1,0:T(8,128)(2,1)} %scale.1.refs_0_.refs_3_), channel_id=1, source_target_pairs={{0,4},{2,6},{4,8},{6,10},{8,12},{10,14},{12,0},{14,2},{1,5},{3,7},... | collective-permute-start | bytes 2359304 | tf_op jit(solution)/shard_map/ppermute | solution.py:246
  7.5 0.0 copy-start
  7.6 1.8 %copy-done = bf16[384,3584]{1,0:T(8,128)(2,1)S(1)} copy-done((bf16[384,3584]{1,0:T(8,128)(2,1)S(1)}, bf16[384,3584]{1,0:T(8,128)(2,1)}, u32[]{:S(2)}) %copy-start) | copy-done | bytes 2752536
  9.3 0.0 copy-start.2
  9.3 3.5 %hidden.1.hidden_ref = bf16[384,3584]{1,0:T(8,128)(2,1)S(1)} custom-call(bf16[384,3584]{1,0:T(8,128)(2,1)S(1)} %copy-done, bf16[384,3584]{1,0:T(8,128)(2,1)} %refs_6_.3), custom_call_target="tpu_custom_call" | custom-call | flops 22020096 | bytes 8257536 | tf_op jit(solution)/shard_map/hidden/pallas_call | solution.py:64
  12.8 0.0 copy-done.2
  12.9 2.3 %collective-permute-start = (bf16[384,1024]{1,0:T(8,128)(2,1)S(1)}, bf16[384,1024]{1,0:T(8,128)(2,1)}, u32[]{:S(2)}, u32[]{:S(2)}) collective-permute-start(bf16[384,1024]{1,0:T(8,128)(2,1)S(1)} %copy-done.2), channel_id=1, source_target_pairs={{0,12},{2,14},{4,0},{6,2},{8,4},{10,6},{12,8},{14,10},{1,13},{3,15... | collective-permute-start | bytes 2359304 | tf_op jit(solution)/shard_map/ppermute | solution.py:246
  15.2 17.8 %moments.2.refs_12_.refs_13_.refs_2_.refs_3_ = f32[4,384,1024]{2,1,0:T(8,128)} custom-call(s32[8]{0:T(128)S(1)} %fusion.3.order_ref, bf16[384,3584]{1,0:T(8,128)(2,1)S(1)} %hidden.1.hidden_ref, s32[3584,4096]{1,0:T(8,128)} %refs_3_.1), custom_call_target="tpu_custom_call" | custom-call | flops 11274289152 | bytes 29360128 | tf_op jit(solution)/shard_map/moments/pallas_call | solution.py:101
  33.0 0.0 collective-permute-done.2.refs_2_.refs_5_
  33.0 0.0 collective-permute-done.1.refs_1_.refs_4_
  33.0 0.1 collective-permute-start.6
  33.0 0.4 collective-permute-start.3
  33.4 18.7 %moments.3 = (f32[4,384,1024]{2,1,0:T(8,128)}, f32[1,1024]{1,0:T(1,128)S(1)}, f32[1,1024]{1,0:T(1,128)S(1)}, f32[1,1024]{1,0:T(1,128)S(1)}) custom-call(s32[8]{0:T(128)S(1)} %fusion.3.order_ref, bf16[384,3584]{1,0:T(8,128)(2,1)S(1)} %hidden.1.hidden_ref, s32[3584,4096]{1,0:T(8,128)} %refs_3_.1, bf16[384,1024]{1,0:T(8,128)(2,1)S(1)} %copy-done.2, ...), custom_call_target="tpu_custom_call" | custom-call | flops 11274289152 | bytes 29360128 | tf_op jit(solution)/shard_map/moments/pallas_call | solution.py:101
  52.1 0.0 collective-permute-done.refs_1_
  52.1 0.0 collective-permute-done.3.refs_2_
  52.1 11.0 %collective-permute-start.4 = (bf16[384,1024]{1,0:T(8,128)(2,1)S(1)}, bf16[384,1024]{1,0:T(8,128)(2,1)S(1)}, u32[]{:S(2)}, u32[]{:S(2)}) collective-permute-start(bf16[384,1024]{1,0:T(8,128)(2,1)S(1)} %collective-permute-done.3.refs_2_), channel_id=1, source_target_pairs={{0,4},{2,6},{4,8},{6,10},{8,12},{10,14},{12,0},{14,2},{1,5},{3,7},... | collective-permute-start | bytes 2359304 | tf_op jit(solution)/shard_map/ppermute | solution.py:246
  63.2 1.5 %collective-permute-start.5 = (bf16[384,1024]{1,0:T(8,128)(2,1)}, bf16[384,1024]{1,0:T(8,128)(2,1)S(1)}, u32[]{:S(2)}, u32[]{:S(2)}) collective-permute-start(bf16[384,1024]{1,0:T(8,128)(2,1)} %collective-permute-done.refs_1_), channel_id=1, source_target_pairs={{0,2},{2,0},{4,6},{6,4},{8,10},{10,8},{12,14},{14,12},{1,3},{3,1},... | collective-permute-start | bytes 2359304 | tf_op jit(solution)/shard_map/ppermute | solution.py:246
  64.7 0.0 collective-permute-done.6.refs_0_
  64.7 26.9 %back.1 = (f32[384,3584]{1,0:T(8,128)}, f32[1,1024]{1,0:T(1,128)S(1)}, f32[1,1024]{1,0:T(1,128)S(1)}, f32[1,1024]{1,0:T(1,128)S(1)}) custom-call(s32[8]{0:T(128)S(1)} %fusion.3.order_ref, bf16[384,1024]{1,0:T(8,128)(2,1)S(1)} %collective-permute-done.6.refs_0_, bf16[384,1024]{1,0:T(8,128)(2,1)} %collective-permute-done.refs_1_, ...), custom_call_target="tpu_custom_call" | custom-call | flops 16911433728 | bytes 44040192 | tf_op jit(solution)/shard_map/back/pallas_call | solution.py:205
  91.6 0.0 collective-permute-done.4.refs_0_
  91.6 0.0 collective-permute-done.5.refs_1_
  91.6 0.0 copy-start.1
  91.6 2.5 %sums.1 = (f32[4,512]{1,0:T(4,128)S(1)}, f32[4,512]{1,0:T(4,128)S(1)}, f32[4,512]{1,0:T(4,128)S(1)}, f32[4,512]{1,0:T(4,128)S(1)}) custom-call(s32[1]{0:T(128)} %bitcast.1.core_ref, bf16[384,1024]{1,0:T(8,128)(2,1)S(1)} %collective-permute-done.4.refs_0_, bf16[384,1024]{1,0:T(8,128)(2,1)S(1)} %collective-permute-done.5.refs_1_, ...), custom_call_target="tpu_custom_call" | custom-call | flops 1572864 | bytes 4718592 | tf_op jit(solution)/shard_map/sums/pallas_call | solution.py:146
  94.2 0.1 collective-permute-start.7
  94.3 0.6 collective-permute-start.8
  94.8 1.3 %collective-permute-start.9 = (f32[4,512]{1,0:T(4,128)S(1)}, f32[4,512]{1,0:T(4,128)S(1)}, u32[]{:S(2)}, u32[]{:S(2)}) collective-permute-start(f32[4,512]{1,0:T(4,128)S(1)} %get-tuple-element.48), channel_id=1, source_target_pairs={{0,3},{1,2},{2,1},{3,0},{4,7},{5,6},{6,5},{7,4},{8,11},{9,10},{10,... | collective-permute-start | bytes 24584 | tf_op jit(solution)/shard_map/ppermute | solution.py:274
  96.1 0.0 collective-permute-done.7
  96.1 1.9 %collective-permute-done.8 = f32[4,512]{1,0:T(4,128)S(1)} collective-permute-done((f32[4,512]{1,0:T(4,128)S(1)}, f32[4,512]{1,0:T(4,128)S(1)}, u32[]{:S(2)}, u32[]{:S(2)}) %collective-permute-start.8) | collective-permute-done | bytes 8224 | tf_op jit(solution)/shard_map/ppermute | solution.py:246
  98.0 0.0 collective-permute-done.9
  98.0 0.7 collective-permute-start.10
  98.8 1.4 %collective-permute-start.12 = (f32[1,512]{1,0:T(1,128)S(1)}, f32[1,512]{1,0:T(1,128)S(1)}, u32[]{:S(2)}, u32[]{:S(2)}) collective-permute-start(f32[1,512]{1,0:T(1,128)S(1)} %get-tuple-element.50), channel_id=1, source_target_pairs={{0,4},{2,6},{4,8},{6,10},{8,12},{10,14},{12,0},{14,2},{1,5},{3,7},... | collective-permute-start | bytes 6152 | tf_op jit(solution)/shard_map/ppermute | solution.py:246
  100.1 1.2 %collective-permute-start.11 = (f32[1,512]{1,0:T(1,128)S(1)}, f32[1,512]{1,0:T(1,128)S(1)}, u32[]{:S(2)}, u32[]{:S(2)}) collective-permute-start(f32[1,512]{1,0:T(1,128)S(1)} %get-tuple-element.51), channel_id=1, source_target_pairs={{0,8},{2,10},{4,12},{6,14},{8,0},{10,2},{12,4},{14,6},{1,9},{3,11}... | collective-permute-start | bytes 6152 | tf_op jit(solution)/shard_map/ppermute | solution.py:246
  101.3 0.0 copy-done.1
  101.3 15.1 %tail.1 = (bf16[384,3584]{1,0:T(8,128)(2,1)}, bf16[384,3584]{1,0:T(8,128)(2,1)}) custom-call(s32[8]{0:T(128)S(1)} %fusion.3.order_ref, bf16[384,1024]{1,0:T(8,128)(2,1)S(1)} %collective-permute-done.4.refs_0_, bf16[384,1024]{1,0:T(8,128)(2,1)S(1)} %collective-permute-done.5.refs_1_, s32[3584,4096]{1,0:T(8,128)} %refs_3_.1, s32[3584,4096]{1,0:T(8,128)} %refs_3_.1, ...), custom_call_target="tpu_custom_call" | custom-call | flops 5637144576 | bytes 14680064 | tf_op jit(solution)/shard_map/tail/pallas_call | solution.py:205
  116.4 0.0 collective-permute-done.10
  116.4 0.0 collective-permute-done.12
  116.4 0.0 collective-permute-done.11
  116.5 0.1 copy.8
  116.6 0.7 reshape.21
  (5 shorter events, 0.1 us)
Async XLA Ops:
  3.0 29.9 %collective-permute-start.2 = (bf16[384,1024]{1,0:T(8,128)(2,1)}, bf16[384,1024]{1,0:T(8,128)(2,1)}, u32[]{:S(2)}, u32[]{:S(2)}) collective-permute-start(bf16[384,1024]{1,0:T(8,128)(2,1)} %scale.1.refs_0_.refs_3_), channel_id=1, source_target_pairs={{0,2},{2,0},{4,6},{6,4},{8,10},{10,8},{12,14},{14,12},{1,3},{3,1},... | collective-permute-start | bytes 2359304 | tf_op jit(solution)/shard_map/ppermute | solution.py:246
  6.0 27.0 %collective-permute-start.1 = (bf16[384,1024]{1,0:T(8,128)(2,1)}, bf16[384,1024]{1,0:T(8,128)(2,1)}, u32[]{:S(2)}, u32[]{:S(2)}) collective-permute-start(bf16[384,1024]{1,0:T(8,128)(2,1)} %scale.1.refs_0_.refs_3_), channel_id=1, source_target_pairs={{0,4},{2,6},{4,8},{6,10},{8,12},{10,14},{12,0},{14,2},{1,5},{3,7},... | collective-permute-start | bytes 2359304 | tf_op jit(solution)/shard_map/ppermute | solution.py:246
  7.5 1.8 %copy-start = (bf16[384,3584]{1,0:T(8,128)(2,1)S(1)}, bf16[384,3584]{1,0:T(8,128)(2,1)}, u32[]{:S(2)}) copy-start(bf16[384,3584]{1,0:T(8,128)(2,1)} %refs_5_.1) | copy-start | bytes 8257540
  9.3 3.5 %copy-start.2 = (bf16[384,1024]{1,0:T(8,128)(2,1)S(1)}, bf16[384,1024]{1,0:T(8,128)(2,1)}, u32[]{:S(2)}) copy-start(bf16[384,1024]{1,0:T(8,128)(2,1)} %scale.1.refs_0_.refs_3_) | copy-start | bytes 2359300
  12.9 39.3 %collective-permute-start = (bf16[384,1024]{1,0:T(8,128)(2,1)S(1)}, bf16[384,1024]{1,0:T(8,128)(2,1)}, u32[]{:S(2)}, u32[]{:S(2)}) collective-permute-start(bf16[384,1024]{1,0:T(8,128)(2,1)S(1)} %copy-done.2), channel_id=1, source_target_pairs={{0,12},{2,14},{4,0},{6,2},{8,4},{10,6},{12,8},{14,10},{1,13},{3,15... | collective-permute-start | bytes 2359304 | tf_op jit(solution)/shard_map/ppermute | solution.py:246
  33.0 31.7 %collective-permute-start.6 = (bf16[384,1024]{1,0:T(8,128)(2,1)}, bf16[384,1024]{1,0:T(8,128)(2,1)S(1)}, u32[]{:S(2)}, u32[]{:S(2)}) collective-permute-start(bf16[384,1024]{1,0:T(8,128)(2,1)} %collective-permute-done.1.refs_1_.refs_4_), channel_id=1, source_target_pairs={{0,4},{2,6},{4,8},{6,10},{8,12},{10,14},{12,0},{14,2},{1,5},{3,7},... | collective-permute-start | bytes 2359304 | tf_op jit(solution)/shard_map/ppermute | solution.py:246
  33.0 19.1 %collective-permute-start.3 = (bf16[384,1024]{1,0:T(8,128)(2,1)}, bf16[384,1024]{1,0:T(8,128)(2,1)S(1)}, u32[]{:S(2)}, u32[]{:S(2)}) collective-permute-start(bf16[384,1024]{1,0:T(8,128)(2,1)} %collective-permute-done.1.refs_1_.refs_4_), channel_id=1, source_target_pairs={{0,2},{2,0},{4,6},{6,4},{8,10},{10,8},{12,14},{14,12},{1,3},{3,1},... | collective-permute-start | bytes 2359304 | tf_op jit(solution)/shard_map/ppermute | solution.py:246
  52.1 39.5 %collective-permute-start.4 = (bf16[384,1024]{1,0:T(8,128)(2,1)S(1)}, bf16[384,1024]{1,0:T(8,128)(2,1)S(1)}, u32[]{:S(2)}, u32[]{:S(2)}) collective-permute-start(bf16[384,1024]{1,0:T(8,128)(2,1)S(1)} %collective-permute-done.3.refs_2_), channel_id=1, source_target_pairs={{0,4},{2,6},{4,8},{6,10},{8,12},{10,14},{12,0},{14,2},{1,5},{3,7},... | collective-permute-start | bytes 2359304 | tf_op jit(solution)/shard_map/ppermute | solution.py:246
  63.2 28.4 %collective-permute-start.5 = (bf16[384,1024]{1,0:T(8,128)(2,1)}, bf16[384,1024]{1,0:T(8,128)(2,1)S(1)}, u32[]{:S(2)}, u32[]{:S(2)}) collective-permute-start(bf16[384,1024]{1,0:T(8,128)(2,1)} %collective-permute-done.refs_1_), channel_id=1, source_target_pairs={{0,2},{2,0},{4,6},{6,4},{8,10},{10,8},{12,14},{14,12},{1,3},{3,1},... | collective-permute-start | bytes 2359304 | tf_op jit(solution)/shard_map/ppermute | solution.py:246
  91.6 9.7 %copy-start.1 = (bf16[384,3584]{1,0:T(8,128)(2,1)S(1)}, bf16[384,3584]{1,0:T(8,128)(2,1)}, u32[]{:S(2)}) copy-start(bf16[384,3584]{1,0:T(8,128)(2,1)} %refs_5_.1) | copy-start | bytes 8257540
  94.2 1.9 %collective-permute-start.7 = (f32[4,512]{1,0:T(4,128)S(1)}, f32[4,512]{1,0:T(4,128)S(1)}, u32[]{:S(2)}, u32[]{:S(2)}) collective-permute-start(f32[4,512]{1,0:T(4,128)S(1)} %get-tuple-element.46), channel_id=1, source_target_pairs={{0,1},{1,0},{2,3},{3,2},{4,5},{5,4},{6,7},{7,6},{8,9},{9,8},{10,11... | collective-permute-start | bytes 24584 | tf_op jit(solution)/shard_map/ppermute | solution.py:273
  94.3 3.8 %collective-permute-start.8 = (f32[4,512]{1,0:T(4,128)S(1)}, f32[4,512]{1,0:T(4,128)S(1)}, u32[]{:S(2)}, u32[]{:S(2)}) collective-permute-start(f32[4,512]{1,0:T(4,128)S(1)} %get-tuple-element.47), channel_id=1, source_target_pairs={{0,2},{2,0},{4,6},{6,4},{8,10},{10,8},{12,14},{14,12},{1,3},{3,1},... | collective-permute-start | bytes 24584 | tf_op jit(solution)/shard_map/ppermute | solution.py:246
  94.8 3.2 %collective-permute-start.9 = (f32[4,512]{1,0:T(4,128)S(1)}, f32[4,512]{1,0:T(4,128)S(1)}, u32[]{:S(2)}, u32[]{:S(2)}) collective-permute-start(f32[4,512]{1,0:T(4,128)S(1)} %get-tuple-element.48), channel_id=1, source_target_pairs={{0,3},{1,2},{2,1},{3,0},{4,7},{5,6},{6,5},{7,4},{8,11},{9,10},{10,... | collective-permute-start | bytes 24584 | tf_op jit(solution)/shard_map/ppermute | solution.py:274
  98.0 18.4 %collective-permute-start.10 = (f32[1,512]{1,0:T(1,128)S(1)}, f32[1,512]{1,0:T(1,128)S(1)}, u32[]{:S(2)}, u32[]{:S(2)}) collective-permute-start(f32[1,512]{1,0:T(1,128)S(1)} %get-tuple-element.49), channel_id=1, source_target_pairs={{0,12},{2,14},{4,0},{6,2},{8,4},{10,6},{12,8},{14,10},{1,13},{3,15... | collective-permute-start | bytes 6152 | tf_op jit(solution)/shard_map/ppermute | solution.py:246
  98.8 17.7 %collective-permute-start.12 = (f32[1,512]{1,0:T(1,128)S(1)}, f32[1,512]{1,0:T(1,128)S(1)}, u32[]{:S(2)}, u32[]{:S(2)}) collective-permute-start(f32[1,512]{1,0:T(1,128)S(1)} %get-tuple-element.50), channel_id=1, source_target_pairs={{0,4},{2,6},{4,8},{6,10},{8,12},{10,14},{12,0},{14,2},{1,5},{3,7},... | collective-permute-start | bytes 6152 | tf_op jit(solution)/shard_map/ppermute | solution.py:246
  100.1 16.3 %collective-permute-start.11 = (f32[1,512]{1,0:T(1,128)S(1)}, f32[1,512]{1,0:T(1,128)S(1)}, u32[]{:S(2)}, u32[]{:S(2)}) collective-permute-start(f32[1,512]{1,0:T(1,128)S(1)} %get-tuple-element.51), channel_id=1, source_target_pairs={{0,8},{2,10},{4,12},{6,14},{8,0},{10,2},{12,4},{14,6},{1,9},{3,11}... | collective-permute-start | bytes 6152 | tf_op jit(solution)/shard_map/ppermute | solution.py:246

commit v3 on v2

--- a/solution.py
+++ b/solution.py
@@ -9,7 +9,8 @@
 
 F32 = jnp.float32
 BF16 = jnp.bfloat16
-VMEM_LIMIT = 48 << 20
+MIB = 1 << 20
+VMEM_MIB = {"hidden": 58, "moments": 50, "back": 46, "sums": 12, "tail": 30}
 
 
 def sigmoid(v):
@@ -68,56 +69,41 @@
         out_specs=spec,
         out_shape=jax.ShapeDtypeStruct((rows, units), BF16),
         name="hidden",
-        compiler_params=pltpu.CompilerParams(vmem_limit_bytes=VMEM_LIMIT),
+        compiler_params=pltpu.CompilerParams(vmem_limit_bytes=VMEM_MIB["hidden"] * MIB),
         cost_estimate=cost(16 * rows * units, 6 * rows * units),
     )(gate, up)
 
 
-def moments_kernel(n_known, order_ref, hidden_ref, words_ref, *refs):
-    grads, out_ref, sums = refs[:n_known], refs[n_known], refs[n_known + 1:]
+def moments_kernel(order_ref, hidden_ref, words_ref, out_ref):
     total = None
     for k in range(0, hidden_ref.shape[1], BLOCK):
         product = jnp.dot(
             hidden_ref[:, k:k + BLOCK], nibbles(words_ref[k:k + BLOCK, :]), preferred_element_type=F32
         )
         total = product if total is None else total + product
-    out_ref[0] = total
-    for s in range(n_known):
-
-        @pl.when(pl.program_id(0) == s)
-        def _(s=s):
-            sums[s][...] = jnp.sum(grads[s][...].astype(F32) * out_ref[0], axis=0, keepdims=True)
-
-
-def moments_call(order, shards, hidden, words, shard_words, grads):
+    out_ref[0] = total.astype(BF16)
+
+
+def moments_call(order, hidden, words, shard_words):
     rows, units = hidden.shape
-    n = len(shards)
-    first, second = shards[0], shards[n // 2]
-
-    def place(s, o):
-        return 0, o[jnp.where(s < n // 2, first + s, second - n // 2 + s)]
-
+    n = order.shape[0]
     width = 2 * shard_words
-    out = pl.pallas_call(
-        functools.partial(moments_kernel, len(grads)),
+    return pl.pallas_call(
+        moments_kernel,
         grid_spec=pltpu.PrefetchScalarGridSpec(
             num_scalar_prefetch=1,
             grid=(n,),
             in_specs=[
-                HELD,
-                pl.BlockSpec((units, shard_words), place),
-            ]
-            + [HELD] * len(grads),
-            out_specs=[pl.BlockSpec((1, rows, width), lambda s, o: (s, 0, 0))]
-            + [pl.BlockSpec((1, width), lambda s, o: (0, 0))] * len(grads),
+                pl.BlockSpec((rows, units), lambda s, o: (0, 0)),
+                pl.BlockSpec((units, shard_words), lambda s, o: (0, o[s])),
+            ],
+            out_specs=pl.BlockSpec((1, rows, width), lambda s, o: (s, 0, 0)),
         ),
-        out_shape=[jax.ShapeDtypeStruct((n, rows, width), F32)]
-        + [jax.ShapeDtypeStruct((1, width), F32)] * len(grads),
+        out_shape=jax.ShapeDtypeStruct((n, rows, width), BF16),
         name="moments",
-        compiler_params=pltpu.CompilerParams(vmem_limit_bytes=VMEM_LIMIT),
+        compiler_params=pltpu.CompilerParams(vmem_limit_bytes=VMEM_MIB["moments"] * MIB),
         cost_estimate=cost(4 * n * rows * units * shard_words, 4 * n * units * shard_words),
-    )(order, hidden, words, *grads)
-    return out[0], out[1:]
+    )(order, hidden, words)
 
 
 BLOCK = 512
@@ -127,7 +113,7 @@
 def sums_kernel(core_ref, *refs):
     grads, moments, known, outs = refs[:2], refs[2:4], refs[4:10], refs[10:]
     late = [
-        jnp.sum(g[...].astype(F32) * m[0], axis=0, keepdims=True) for g, m in zip(grads, moments)
+        jnp.sum(g[...].astype(F32) * m[0].astype(F32), axis=0, keepdims=True) for g, m in zip(grads, moments)
     ]
     rows = [ref[...] for ref in known] + late
     quarter = rows[0].shape[1] // 4
@@ -155,7 +141,7 @@
         ),
         out_shape=[jax.ShapeDtypeStruct((4, width // 2), F32)] * 4,
         name="sums",
-        compiler_params=pltpu.CompilerParams(vmem_limit_bytes=VMEM_LIMIT),
+        compiler_params=pltpu.CompilerParams(vmem_limit_bytes=VMEM_MIB["sums"] * MIB),
         cost_estimate=cost(2 * n * rows * width, 6 * n * rows * width),
     )(core.reshape(1).astype(jnp.int32), *grads, *([moments] * n), *known)
 
@@ -185,7 +171,7 @@
     def _():
         part = pl.ds(pl.multiple_of(step * rows, rows), rows)
         for s in range(n_sums):
-            terms = grads[s][part, :].astype(F32) * moments[s][0]
+            terms = grads[s][part, :].astype(F32) * moments[s][0].astype(F32)
             sums[s][...] += jnp.sum(terms, axis=0, keepdims=True)
 
 
@@ -213,7 +199,7 @@
         out_shape=[jax.ShapeDtypeStruct((rows, units), kind) for kind in wide_out]
         + [jax.ShapeDtypeStruct((1, width), F32)] * len(moments),
         name=name,
-        compiler_params=pltpu.CompilerParams(vmem_limit_bytes=VMEM_LIMIT),
+        compiler_params=pltpu.CompilerParams(vmem_limit_bytes=VMEM_MIB[name] * MIB),
         cost_estimate=cost(2 * n * rows * units * width, 2 * n * units * width),
     )(order, *grads, *([words] * n), *[m for m, _ in moments], *wide_in)
     return out[:len(wide_out)], out[len(wide_out):]
@@ -221,6 +207,10 @@
 
 def back(product, total_ref):
     total_ref[...] = product
+
+
+def back_more(product, before_ref, total_ref):
+    total_ref[...] = before_ref[...] + product
 
 
 def tail(product, before_ref, gate_ref, up_ref, gate_out_ref, up_out_ref):
@@ -254,20 +244,23 @@
     hidden = hidden_call(gate, up)
     own, hidden = together((own, hidden))
     line3 = move(own, -1)
-    m_later, _ = moments_call(order, [2, 3, 6, 7], hidden, words, shard_words, [])
-    line1, cross0, m_later, hidden = together((line1, cross0, m_later, hidden))
+    moments = moments_call(order, hidden, words, shard_words)
+    line1, cross0, line3, moments = together((line1, cross0, line3, moments))
     line2 = move(line1, 1)
     cross1 = move(line1, 0, 1)
-    m_soon, (s0, s1, c0) = moments_call(order, [0, 1, 4, 5], hidden, words, shard_words, [own, line1, cross0])
-    line3, cross1, m_soon = together((line3, cross1, m_soon))
+    (total,), (s1, s3, c0) = product_call(
+        "back", back, order, words, [1, 3, 4], [line1, line3, cross0], [(moments, s) for s in (1, 3, 4)], [], [F32]
+    )
+    cross1, total = together((cross1, total))
     cross2 = move(cross1, 1)
     cross3 = move(line3, 0, 1)
-    (total,), (s2, s3, c1) = product_call(
-        "back", back, order, words, [2, 3, 5, 0, 1, 4], [line2, line3, cross1, own, line1, cross0],
-        [(m_later, 0), (m_later, 1), (m_soon, 3)], [], [F32],
-    )
+    (total,), (s0, s2, c1) = product_call(
+        "back", back_more, order, words, [0, 2, 5], [own, line2, cross1],
+        [(moments, s) for s in (0, 2, 5)], [total], [F32],
+    )
+
     lines, lines_other, crossed, crossed_other = sums_call(
-        core, m_later, [2, 3], [cross2, cross3], [s0, s1, s2, s3, c0, c1]
+        core, moments, [6, 7], [cross2, cross3], [s0, s1, s2, s3, c0, c1]
     )
     diagonal = [(2 * a + c, 2 * b + 1 - c) for a, b in shifted(0, 1) for c in (0, 1)]
     lines = lines + lax.ppermute(lines_other, "seq", [(0, 1), (1, 0)])

time: 118 us -> 110 us (0.932)
  starting transfers between devices: 25 us -> 16.4 us
  Pallas kernels: 87 us -> 82.5 us
  local copies, waits for them, and re-layouts: 2.67 us -> 5.08 us
  waiting for transfers between devices: 1.92 us -> 4.3 us
    ppermute x11, starting transfers between devices: 23.7 us -> 15.1 us  [move(): return lax.ppermute(v, 'tp', shifted(step, flip))]
    pallas_call x2 -> x1, Pallas kernels: 36.5 us -> 30.1 us  [moments_call(): pl.pallas_call(moments_kernel, grid_spec=pltpu.PrefetchScalarGridSpec(num...]
    pallas_call x2 -> x3, Pallas kernels: 42 us -> 44.6 us  [product_call(): pl.pallas_call(functools.partial(product_kernel, n, len(moments), finish)...]
    unnamed x6 -> x14, local copies, waits for them, and re-layouts: 1.79 us -> 4.19 us
    ppermute x11, waiting for transfers between devices: 1.92 us -> 4.29 us  [move(): return lax.ppermute(v, 'tp', shifted(step, flip))]
    pallas_call x1, Pallas kernels: 2.55 us -> 0.18 us  [sums_call(): pl.pallas_call(sums_kernel, grid_spec=pltpu.PrefetchScalarGridSpec(num_sc...]
    pallas_call x1, Pallas kernels: 3.51 us -> 5.23 us  [hidden_call(): pl.pallas_call(hidden_kernel, grid=(rows // 96,), in_specs=[spec, spec],...]
  transfers between devices with their start and end apart: 13 -> 13, of which waited for: 1 -> 3; matrix products, arithmetic and copies ran while one was open for 0% -> 0% of each run, Pallas kernels for 70% -> 73%
where the time goes in v3:
time: 110 us; the launch traced here: 109 us
  Pallas kernels  82.5 us (75%)
  starting transfers between devices  16.4 us (15%)
  local copies, waits for them, and re-layouts  5.08 us (5%)
  waiting for transfers between devices  4.3 us (4%)
    pallas_call x3, Pallas kernels, product_call(): pl.pallas_call(functools.partial(product_kernel, n, len(moments), finish)...  44.6 us
    pallas_call x1, Pallas kernels, moments_call(): pl.pallas_call(moments_kernel, grid_spec=pltpu.PrefetchScalarGridSpec(num...  30.1 us
    ppermute x11, starting transfers between devices, move(): return lax.ppermute(v, 'tp', shifted(step, flip))  15.1 us
    pallas_call x1, Pallas kernels, hidden_call(): pl.pallas_call(hidden_kernel, grid=(rows // 96,), in_specs=[spec, spec],...  5.23 us
    ppermute x11, waiting for transfers between devices, move(): return lax.ppermute(v, 'tp', shifted(step, flip))  4.29 us
    unnamed x14, local copies, waits for them, and re-layouts  4.19 us
    pallas_call x1, Pallas kernels, scale_call(): pl.pallas_call(scale_kernel, out_shape=jax.ShapeDtypeStruct((rows, width)...  2.4 us
  transfers between devices with their start and end apart: 13, of which 3 were waited for; matrix products, arithmetic and copies ran while one was open for 0% of the time, Pallas kernels for 73%

profile of v3, /device:TPU:0, one launch (start us, length us, event | category | flops | bytes accessed | tf_op | source)
XLA Modules:
  0.0 109.1 jit_solution(8088776413921558022)
XLA Ops:
  0.6 2.4 %scale.1.refs_0_ = bf16[384,1024]{1,0:T(8,128)(2,1)} custom-call(bf16[384,1024]{1,0:T(8,128)(2,1)} %grad_ref.1, f32[1,1024]{1,0:T(1,128)} %bitcast.6), custom_call_target="tpu_custom_call" | custom-call | flops 201326592 | bytes 1572864 | tf_op jit(solution)/shard_map/scale/pallas_call | solution.py:49
  3.0 0.0 copy-start.3
  3.0 2.9 %collective-permute-start.1 = (bf16[384,1024]{1,0:T(8,128)(2,1)}, bf16[384,1024]{1,0:T(8,128)(2,1)S(1)}, u32[]{:S(2)}, u32[]{:S(2)}) collective-permute-start(bf16[384,1024]{1,0:T(8,128)(2,1)} %scale.1.refs_0_), channel_id=1, source_target_pairs={{0,2},{2,0},{4,6},{6,4},{8,10},{10,8},{12,14},{14,12},{1,3},{3,1},... | collective-permute-start | bytes 2359304 | tf_op jit(solution)/shard_map/ppermute | solution.py:236
  6.0 1.6 %collective-permute-start = (bf16[384,1024]{1,0:T(8,128)(2,1)}, bf16[384,1024]{1,0:T(8,128)(2,1)S(1)}, u32[]{:S(2)}, u32[]{:S(2)}) collective-permute-start(bf16[384,1024]{1,0:T(8,128)(2,1)} %scale.1.refs_0_), channel_id=1, source_target_pairs={{0,4},{2,6},{4,8},{6,10},{8,12},{10,14},{12,0},{14,2},{1,5},{3,7},... | collective-permute-start | bytes 2359304 | tf_op jit(solution)/shard_map/ppermute | solution.py:236
  7.6 5.2 %hidden.1.hidden_ref = bf16[384,3584]{1,0:T(8,128)(2,1)} custom-call(bf16[384,3584]{1,0:T(8,128)(2,1)} %refs_5_.5, bf16[384,3584]{1,0:T(8,128)(2,1)} %refs_6_.1), custom_call_target="tpu_custom_call" | custom-call | flops 22020096 | bytes 8257536 | tf_op jit(solution)/shard_map/hidden/pallas_call | solution.py:65
  12.8 0.0 copy-done.3
  12.8 2.2 %collective-permute-start.2 = (bf16[384,1024]{1,0:T(8,128)(2,1)S(1)}, bf16[384,1024]{1,0:T(8,128)(2,1)S(1)}, u32[]{:S(2)}, u32[]{:S(2)}) collective-permute-start(bf16[384,1024]{1,0:T(8,128)(2,1)S(1)} %copy-done.3), channel_id=1, source_target_pairs={{0,12},{2,14},{4,0},{6,2},{8,4},{10,6},{12,8},{14,10},{1,13},{3,15... | collective-permute-start | bytes 2359304 | tf_op jit(solution)/shard_map/ppermute | solution.py:236
  15.0 0.0 copy-start.4
  15.1 1.8 %copy-done.4 = bf16[384,3584]{1,0:T(8,128)(2,1)S(1)} copy-done((bf16[384,3584]{1,0:T(8,128)(2,1)S(1)}, bf16[384,3584]{1,0:T(8,128)(2,1)}, u32[]{:S(2)}) %copy-start.4) | copy-done | bytes 2752536
  16.8 30.1 %moments.1.refs_6_.refs_7_.refs_8_.refs_2_.refs_3_ = bf16[8,384,1024]{2,1,0:T(8,128)(2,1)} custom-call(s32[8]{0:T(128)S(1)} %fusion.3.order_ref, bf16[384,3584]{1,0:T(8,128)(2,1)S(1)} %copy-done.4, s32[3584,4096]{1,0:T(8,128)} %refs_3_.5), custom_call_target="tpu_custom_call" | custom-call | flops 22548578304 | bytes 58720256 | tf_op jit(solution)/shard_map/moments/pallas_call | solution.py:91
  46.9 0.0 collective-permute-done.1.refs_2_
  46.9 0.0 collective-permute-done.refs_0_
  46.9 0.0 collective-permute-done.2.refs_1_
  46.9 0.1 collective-permute-start.6
  47.0 0.4 collective-permute-start.3
  47.4 1.7 %collective-permute-start.5 = (bf16[384,1024]{1,0:T(8,128)(2,1)S(1)}, bf16[384,1024]{1,0:T(8,128)(2,1)S(1)}, u32[]{:S(2)}, u32[]{:S(2)}) collective-permute-start(bf16[384,1024]{1,0:T(8,128)(2,1)S(1)} %collective-permute-done.2.refs_1_), channel_id=1, source_target_pairs={{0,2},{2,0},{4,6},{6,4},{8,10},{10,8},{12,14},{14,12},{1,3},{3,1},... | collective-permute-start | bytes 2359304 | tf_op jit(solution)/shard_map/ppermute | solution.py:236
  49.1 14.5 %back.2 = (f32[384,3584]{1,0:T(8,128)S(1)}, f32[1,1024]{1,0:T(1,128)S(1)}, f32[1,1024]{1,0:T(1,128)S(1)}, f32[1,1024]{1,0:T(1,128)S(1)}) custom-call(s32[8]{0:T(128)S(1)} %fusion.3.order_ref, bf16[384,1024]{1,0:T(8,128)(2,1)S(1)} %collective-permute-done.refs_0_, bf16[384,1024]{1,0:T(8,128)(2,1)S(1)} %collective-permute-done.2.refs_1_, ...), custom_call_target="tpu_custom_call" | custom-call | flops 8455716864 | bytes 22020096 | tf_op jit(solution)/shard_map/back/pallas_call | solution.py:191
  63.6 0.0 copy-start.2
  63.6 2.4 %copy-done.2 = f32[384,3584]{1,0:T(8,128)} copy-done((f32[384,3584]{1,0:T(8,128)}, f32[384,3584]{1,0:T(8,128)S(1)}, u32[]{:S(2)}) %copy-start.2) | copy-done | bytes 5505048
  66.0 1.6 %collective-permute-done.3.refs_2_ = bf16[384,1024]{1,0:T(8,128)(2,1)} collective-permute-done((bf16[384,1024]{1,0:T(8,128)(2,1)S(1)}, bf16[384,1024]{1,0:T(8,128)(2,1)}, u32[]{:S(2)}, u32[]{:S(2)}) %collective-permute-start.3) | collective-permute-done | bytes 786464 | tf_op jit(solution)/shard_map/ppermute | solution.py:236
  67.6 0.0 slice-start
  67.6 0.0 slice-start.1
  67.6 1.3 %collective-permute-start.4 = (bf16[384,1024]{1,0:T(8,128)(2,1)}, bf16[384,1024]{1,0:T(8,128)(2,1)S(1)}, u32[]{:S(2)}, u32[]{:S(2)}) collective-permute-start(bf16[384,1024]{1,0:T(8,128)(2,1)} %collective-permute-done.3.refs_2_), channel_id=1, source_target_pairs={{0,4},{2,6},{4,8},{6,10},{8,12},{10,14},{12,0},{14,2},{1,5},{3,7},... | collective-permute-start | bytes 2359304 | tf_op jit(solution)/shard_map/ppermute | solution.py:236
  68.9 0.0 collective-permute-done.6.refs_1_
  68.9 16.3 %back.3 = (f32[384,3584]{1,0:T(8,128)S(1)}, f32[1,1024]{1,0:T(1,128)S(1)}, f32[1,1024]{1,0:T(1,128)S(1)}, f32[1,1024]{1,0:T(1,128)S(1)}) custom-call(s32[8]{0:T(128)S(1)} %fusion.3.order_ref, bf16[384,1024]{1,0:T(8,128)(2,1)S(1)} %copy-done.3, bf16[384,1024]{1,0:T(8,128)(2,1)S(1)} %collective-permute-done.6.refs_1_, ...), custom_call_target="tpu_custom_call" | custom-call | flops 8455716864 | bytes 22020096 | tf_op jit(solution)/shard_map/back/pallas_call | solution.py:191
  85.2 0.0 collective-permute-done.5.refs_1_
  85.2 0.8 collective-permute-done.4.refs_0_
  86.0 0.0 slice-done
  86.0 0.0 slice-done.1
  86.0 0.0 copy-start.1
  86.0 0.2 sums.1
  86.2 0.1 collective-permute-start.7
  86.3 0.6 collective-permute-start.8
  86.9 1.3 %collective-permute-start.9 = (f32[4,512]{1,0:T(4,128)S(1)}, f32[4,512]{1,0:T(4,128)S(1)}, u32[]{:S(2)}, u32[]{:S(2)}) collective-permute-start(f32[4,512]{1,0:T(4,128)S(1)} %get-tuple-element.46), channel_id=1, source_target_pairs={{0,3},{1,2},{2,1},{3,0},{4,7},{5,6},{6,5},{7,4},{8,11},{9,10},{10,... | collective-permute-start | bytes 24584 | tf_op jit(solution)/shard_map/ppermute | solution.py:267
  88.1 0.0 collective-permute-done.7
  88.1 1.9 %collective-permute-done.8 = f32[4,512]{1,0:T(4,128)S(1)} collective-permute-done((f32[4,512]{1,0:T(4,128)S(1)}, f32[4,512]{1,0:T(4,128)S(1)}, u32[]{:S(2)}, u32[]{:S(2)}) %collective-permute-start.8) | collective-permute-done | bytes 8224 | tf_op jit(solution)/shard_map/ppermute | solution.py:236
  90.0 0.0 collective-permute-done.9
  90.1 2.1 %collective-permute-start.10 = (f32[1,512]{1,0:T(1,128)S(1)}, f32[1,512]{1,0:T(1,128)S(1)}, u32[]{:S(2)}, u32[]{:S(2)}) collective-permute-start(f32[1,512]{1,0:T(1,128)S(1)} %get-tuple-element.47), channel_id=1, source_target_pairs={{0,12},{2,14},{4,0},{6,2},{8,4},{10,6},{12,8},{14,10},{1,13},{3,15... | collective-permute-start | bytes 6152 | tf_op jit(solution)/shard_map/ppermute | solution.py:236
  92.2 0.0 collective-permute-start.12
  92.2 2.2 %collective-permute-start.11 = (f32[1,512]{1,0:T(1,128)S(1)}, f32[1,512]{1,0:T(1,128)S(1)}, u32[]{:S(2)}, u32[]{:S(2)}) collective-permute-start(f32[1,512]{1,0:T(1,128)S(1)} %get-tuple-element.49), channel_id=1, source_target_pairs={{0,8},{2,10},{4,12},{6,14},{8,0},{10,2},{12,4},{14,6},{1,9},{3,11}... | collective-permute-start | bytes 6152 | tf_op jit(solution)/shard_map/ppermute | solution.py:236
  94.4 0.0 copy-done
  94.4 0.0 copy-done.1
  94.4 13.7 %tail.1 = (bf16[384,3584]{1,0:T(8,128)(2,1)}, bf16[384,3584]{1,0:T(8,128)(2,1)}) custom-call(s32[8]{0:T(128)S(1)} %fusion.3.order_ref, bf16[384,1024]{1,0:T(8,128)(2,1)S(1)} %collective-permute-done.4.refs_0_, bf16[384,1024]{1,0:T(8,128)(2,1)S(1)} %collective-permute-done.5.refs_1_, s32[3584,4096]{1,0:T(8,128)} %refs_3_.5, s32[3584,4096]{1,0:T(8,128)} %refs_3_.5, ...), custom_call_target="tpu_custom_call" | custom-call | flops 5637144576 | bytes 14680064 | tf_op jit(solution)/shard_map/tail/pallas_call | solution.py:191
  108.1 0.0 collective-permute-done.10
  108.1 0.0 collective-permute-done.12
  108.1 0.0 collective-permute-done.11
  108.2 0.1 copy.8
  108.3 0.7 reshape.21
  (7 shorter events, 0.1 us)
Async XLA Ops:
  3.0 9.7 %copy-start.3 = (bf16[384,1024]{1,0:T(8,128)(2,1)S(1)}, bf16[384,1024]{1,0:T(8,128)(2,1)}, u32[]{:S(2)}) copy-start(bf16[384,1024]{1,0:T(8,128)(2,1)} %scale.1.refs_0_) | copy-start | bytes 2359300
  3.0 43.9 %collective-permute-start.1 = (bf16[384,1024]{1,0:T(8,128)(2,1)}, bf16[384,1024]{1,0:T(8,128)(2,1)S(1)}, u32[]{:S(2)}, u32[]{:S(2)}) collective-permute-start(bf16[384,1024]{1,0:T(8,128)(2,1)} %scale.1.refs_0_), channel_id=1, source_target_pairs={{0,2},{2,0},{4,6},{6,4},{8,10},{10,8},{12,14},{14,12},{1,3},{3,1},... | collective-permute-start | bytes 2359304 | tf_op jit(solution)/shard_map/ppermute | solution.py:236
  6.0 40.9 %collective-permute-start = (bf16[384,1024]{1,0:T(8,128)(2,1)}, bf16[384,1024]{1,0:T(8,128)(2,1)S(1)}, u32[]{:S(2)}, u32[]{:S(2)}) collective-permute-start(bf16[384,1024]{1,0:T(8,128)(2,1)} %scale.1.refs_0_), channel_id=1, source_target_pairs={{0,4},{2,6},{4,8},{6,10},{8,12},{10,14},{12,0},{14,2},{1,5},{3,7},... | collective-permute-start | bytes 2359304 | tf_op jit(solution)/shard_map/ppermute | solution.py:236
  12.8 34.1 %collective-permute-start.2 = (bf16[384,1024]{1,0:T(8,128)(2,1)S(1)}, bf16[384,1024]{1,0:T(8,128)(2,1)S(1)}, u32[]{:S(2)}, u32[]{:S(2)}) collective-permute-start(bf16[384,1024]{1,0:T(8,128)(2,1)S(1)} %copy-done.3), channel_id=1, source_target_pairs={{0,12},{2,14},{4,0},{6,2},{8,4},{10,6},{12,8},{14,10},{1,13},{3,15... | collective-permute-start | bytes 2359304 | tf_op jit(solution)/shard_map/ppermute | solution.py:236
  15.0 1.8 %copy-start.4 = (bf16[384,3584]{1,0:T(8,128)(2,1)S(1)}, bf16[384,3584]{1,0:T(8,128)(2,1)}, u32[]{:S(2)}) copy-start(bf16[384,3584]{1,0:T(8,128)(2,1)} %hidden.1.hidden_ref) | copy-start | bytes 8257540
  46.9 22.0 %collective-permute-start.6 = (bf16[384,1024]{1,0:T(8,128)(2,1)S(1)}, bf16[384,1024]{1,0:T(8,128)(2,1)S(1)}, u32[]{:S(2)}, u32[]{:S(2)}) collective-permute-start(bf16[384,1024]{1,0:T(8,128)(2,1)S(1)} %collective-permute-done.refs_0_), channel_id=1, source_target_pairs={{0,4},{2,6},{4,8},{6,10},{8,12},{10,14},{12,0},{14,2},{1,5},{3,7},... | collective-permute-start | bytes 2359304 | tf_op jit(solution)/shard_map/ppermute | solution.py:236
  47.0 20.7 %collective-permute-start.3 = (bf16[384,1024]{1,0:T(8,128)(2,1)S(1)}, bf16[384,1024]{1,0:T(8,128)(2,1)}, u32[]{:S(2)}, u32[]{:S(2)}) collective-permute-start(bf16[384,1024]{1,0:T(8,128)(2,1)S(1)} %collective-permute-done.refs_0_), channel_id=1, source_target_pairs={{0,2},{2,0},{4,6},{6,4},{8,10},{10,8},{12,14},{14,12},{1,3},{3,1},... | collective-permute-start | bytes 2359304 | tf_op jit(solution)/shard_map/ppermute | solution.py:236
  47.4 37.8 %collective-permute-start.5 = (bf16[384,1024]{1,0:T(8,128)(2,1)S(1)}, bf16[384,1024]{1,0:T(8,128)(2,1)S(1)}, u32[]{:S(2)}, u32[]{:S(2)}) collective-permute-start(bf16[384,1024]{1,0:T(8,128)(2,1)S(1)} %collective-permute-done.2.refs_1_), channel_id=1, source_target_pairs={{0,2},{2,0},{4,6},{6,4},{8,10},{10,8},{12,14},{14,12},{1,3},{3,1},... | collective-permute-start | bytes 2359304 | tf_op jit(solution)/shard_map/ppermute | solution.py:236
  63.6 2.4 %copy-start.2 = (f32[384,3584]{1,0:T(8,128)}, f32[384,3584]{1,0:T(8,128)S(1)}, u32[]{:S(2)}) copy-start(f32[384,3584]{1,0:T(8,128)S(1)} %get-tuple-element.33.refs_9_) | copy-start | bytes 16515076
  67.6 18.3 %slice-start = ((s8[6291456]{0:T(1024)(128)(4,1)}), s8[4194304]{0:T(1024)(128)(4,1)S(1)}, s32[]{:S(2)}) async-start(s8[6291456]{0:T(1024)(128)(4,1)} %bitcast.3), calls=%async_computation | async-start | bytes 8388608
  67.6 18.3 %slice-start.1 = ((s8[6291456]{0:T(1024)(128)(4,1)}), s8[2097152]{0:T(1024)(128)(4,1)S(1)}, s32[]{:S(2)}) async-start(s8[6291456]{0:T(1024)(128)(4,1)} %bitcast.3), calls=%async_computation.1 | async-start | bytes 4194304
  67.6 18.3 %collective-permute-start.4 = (bf16[384,1024]{1,0:T(8,128)(2,1)}, bf16[384,1024]{1,0:T(8,128)(2,1)S(1)}, u32[]{:S(2)}, u32[]{:S(2)}) collective-permute-start(bf16[384,1024]{1,0:T(8,128)(2,1)} %collective-permute-done.3.refs_2_), channel_id=1, source_target_pairs={{0,4},{2,6},{4,8},{6,10},{8,12},{10,14},{12,0},{14,2},{1,5},{3,7},... | collective-permute-start | bytes 2359304 | tf_op jit(solution)/shard_map/ppermute | solution.py:236
  86.0 8.4 %copy-start = (bf16[384,3584]{1,0:T(8,128)(2,1)S(1)}, bf16[384,3584]{1,0:T(8,128)(2,1)}, u32[]{:S(2)}) copy-start(bf16[384,3584]{1,0:T(8,128)(2,1)} %refs_5_.5) | copy-start | bytes 8257540
  86.0 8.4 %copy-start.1 = (bf16[384,3584]{1,0:T(8,128)(2,1)S(1)}, bf16[384,3584]{1,0:T(8,128)(2,1)}, u32[]{:S(2)}) copy-start(bf16[384,3584]{1,0:T(8,128)(2,1)} %refs_6_.1) | copy-start | bytes 8257540
  86.2 1.9 %collective-permute-start.7 = (f32[4,512]{1,0:T(4,128)S(1)}, f32[4,512]{1,0:T(4,128)S(1)}, u32[]{:S(2)}, u32[]{:S(2)}) collective-permute-start(f32[4,512]{1,0:T(4,128)S(1)} %get-tuple-element.44), channel_id=1, source_target_pairs={{0,1},{1,0},{2,3},{3,2},{4,5},{5,4},{6,7},{7,6},{8,9},{9,8},{10,11... | collective-permute-start | bytes 24584 | tf_op jit(solution)/shard_map/ppermute | solution.py:266
  86.3 3.8 %collective-permute-start.8 = (f32[4,512]{1,0:T(4,128)S(1)}, f32[4,512]{1,0:T(4,128)S(1)}, u32[]{:S(2)}, u32[]{:S(2)}) collective-permute-start(f32[4,512]{1,0:T(4,128)S(1)} %get-tuple-element.45), channel_id=1, source_target_pairs={{0,2},{2,0},{4,6},{6,4},{8,10},{10,8},{12,14},{14,12},{1,3},{3,1},... | collective-permute-start | bytes 24584 | tf_op jit(solution)/shard_map/ppermute | solution.py:236
  86.9 3.2 %collective-permute-start.9 = (f32[4,512]{1,0:T(4,128)S(1)}, f32[4,512]{1,0:T(4,128)S(1)}, u32[]{:S(2)}, u32[]{:S(2)}) collective-permute-start(f32[4,512]{1,0:T(4,128)S(1)} %get-tuple-element.46), channel_id=1, source_target_pairs={{0,3},{1,2},{2,1},{3,0},{4,7},{5,6},{6,5},{7,4},{8,11},{9,10},{10,... | collective-permute-start | bytes 24584 | tf_op jit(solution)/shard_map/ppermute | solution.py:267
  90.1 18.1 %collective-permute-start.10 = (f32[1,512]{1,0:T(1,128)S(1)}, f32[1,512]{1,0:T(1,128)S(1)}, u32[]{:S(2)}, u32[]{:S(2)}) collective-permute-start(f32[1,512]{1,0:T(1,128)S(1)} %get-tuple-element.47), channel_id=1, source_target_pairs={{0,12},{2,14},{4,0},{6,2},{8,4},{10,6},{12,8},{14,10},{1,13},{3,15... | collective-permute-start | bytes 6152 | tf_op jit(solution)/shard_map/ppermute | solution.py:236
  92.2 16.0 %collective-permute-start.12 = (f32[1,512]{1,0:T(1,128)S(1)}, f32[1,512]{1,0:T(1,128)S(1)}, u32[]{:S(2)}, u32[]{:S(2)}) collective-permute-start(f32[1,512]{1,0:T(1,128)S(1)} %get-tuple-element.48), channel_id=1, source_target_pairs={{0,4},{2,6},{4,8},{6,10},{8,12},{10,14},{12,0},{14,2},{1,5},{3,7},... | collective-permute-start | bytes 6152 | tf_op jit(solution)/shard_map/ppermute | solution.py:236
  92.2 16.0 %collective-permute-start.11 = (f32[1,512]{1,0:T(1,128)S(1)}, f32[1,512]{1,0:T(1,128)S(1)}, u32[]{:S(2)}, u32[]{:S(2)}) collective-permute-start(f32[1,512]{1,0:T(1,128)S(1)} %get-tuple-element.49), channel_id=1, source_target_pairs={{0,8},{2,10},{4,12},{6,14},{8,0},{10,2},{12,4},{14,6},{1,9},{3,11}... | collective-permute-start | bytes 6152 | tf_op jit(solution)/shard_map/ppermute | solution.py:236

commit v4 on v3

--- a/solution.py
+++ b/solution.py
@@ -10,7 +10,7 @@
 F32 = jnp.float32
 BF16 = jnp.bfloat16
 MIB = 1 << 20
-VMEM_MIB = {"hidden": 58, "moments": 50, "back": 46, "sums": 12, "tail": 30}
+VMEM_MIB = {"hidden": 58, "moments": 60, "back": 46, "sums": 12, "tail": 30}
 
 
 def sigmoid(v):
@@ -61,10 +61,10 @@
 
 def hidden_call(gate, up):
     rows, units = gate.shape
-    spec = pl.BlockSpec((96, units), lambda i: (i, 0))
+    spec = pl.BlockSpec((64, units), lambda i: (i, 0))
     return pl.pallas_call(
         hidden_kernel,
-        grid=(rows // 96,),
+        grid=(rows // 64,),
         in_specs=[spec, spec],
         out_specs=spec,
         out_shape=jax.ShapeDtypeStruct((rows, units), BF16),

time: 110 us -> 111 us (level)
  Pallas kernels: 82.5 us -> 84.5 us
  local copies, waits for them, and re-layouts: 5.08 us -> 3.31 us
    unnamed x14, local copies, waits for them, and re-layouts: 4.19 us -> 2.42 us
  transfers between devices with their start and end apart: 13 -> 13, of which waited for: 3 -> 3; matrix products, arithmetic and copies ran while one was open for 0% -> 0% of each run, Pallas kernels for 73% -> 75%
where the time goes in v4:
time: 111 us; the launch traced here: 110 us
  Pallas kernels  84.5 us (76%)
  starting transfers between devices  16.4 us (15%)
  waiting for transfers between devices  4.29 us (4%)
  local copies, waits for them, and re-layouts  3.31 us (3%)
    pallas_call x3, Pallas kernels, product_call(): pl.pallas_call(functools.partial(product_kernel, n, len(moments), finish)...  44.6 us
    pallas_call x1, Pallas kernels, moments_call(): pl.pallas_call(moments_kernel, grid_spec=pltpu.PrefetchScalarGridSpec(num...  31.2 us
    ppermute x11, starting transfers between devices, move(): return lax.ppermute(v, 'tp', shifted(step, flip))  15.1 us
    pallas_call x1, Pallas kernels, hidden_call(): pl.pallas_call(hidden_kernel, grid=(rows // 64,), in_specs=[spec, spec],...  6.18 us
    ppermute x11, waiting for transfers between devices, move(): return lax.ppermute(v, 'tp', shifted(step, flip))  4.29 us
    unnamed x14, local copies, waits for them, and re-layouts  2.42 us
    pallas_call x1, Pallas kernels, scale_call(): pl.pallas_call(scale_kernel, out_shape=jax.ShapeDtypeStruct((rows, width)...  2.4 us
  transfers between devices with their start and end apart: 13, of which 3 were waited for; matrix products, arithmetic and copies ran while one was open for 0% of the time, Pallas kernels for 75%

profile of v4, /device:TPU:0, one launch (start us, length us, event | category | flops | bytes accessed | tf_op | source)
XLA Modules:
  0.0 109.8 jit_solution(72748772756426088)
XLA Ops:
  0.6 2.4 %scale.1.refs_0_ = bf16[384,1024]{1,0:T(8,128)(2,1)} custom-call(bf16[384,1024]{1,0:T(8,128)(2,1)} %grad_ref.1, f32[1,1024]{1,0:T(1,128)} %bitcast.6), custom_call_target="tpu_custom_call" | custom-call | flops 201326592 | bytes 1572864 | tf_op jit(solution)/shard_map/scale/pallas_call | solution.py:49
  3.0 0.0 copy-start.3
  3.0 2.9 %collective-permute-start.1 = (bf16[384,1024]{1,0:T(8,128)(2,1)}, bf16[384,1024]{1,0:T(8,128)(2,1)S(1)}, u32[]{:S(2)}, u32[]{:S(2)}) collective-permute-start(bf16[384,1024]{1,0:T(8,128)(2,1)} %scale.1.refs_0_), channel_id=1, source_target_pairs={{0,2},{2,0},{4,6},{6,4},{8,10},{10,8},{12,14},{14,12},{1,3},{3,1},... | collective-permute-start | bytes 2359304 | tf_op jit(solution)/shard_map/ppermute | solution.py:236
  6.0 1.6 %collective-permute-start = (bf16[384,1024]{1,0:T(8,128)(2,1)}, bf16[384,1024]{1,0:T(8,128)(2,1)S(1)}, u32[]{:S(2)}, u32[]{:S(2)}) collective-permute-start(bf16[384,1024]{1,0:T(8,128)(2,1)} %scale.1.refs_0_), channel_id=1, source_target_pairs={{0,4},{2,6},{4,8},{6,10},{8,12},{10,14},{12,0},{14,2},{1,5},{3,7},... | collective-permute-start | bytes 2359304 | tf_op jit(solution)/shard_map/ppermute | solution.py:236
  7.6 6.2 %hidden.1.hidden_ref = bf16[384,3584]{1,0:T(8,128)(2,1)} custom-call(bf16[384,3584]{1,0:T(8,128)(2,1)} %refs_5_.5, bf16[384,3584]{1,0:T(8,128)(2,1)} %refs_6_.1), custom_call_target="tpu_custom_call" | custom-call | flops 22020096 | bytes 8257536 | tf_op jit(solution)/shard_map/hidden/pallas_call | solution.py:65
  13.7 0.0 copy-done.3
  13.7 2.2 %collective-permute-start.2 = (bf16[384,1024]{1,0:T(8,128)(2,1)S(1)}, bf16[384,1024]{1,0:T(8,128)(2,1)S(1)}, u32[]{:S(2)}, u32[]{:S(2)}) collective-permute-start(bf16[384,1024]{1,0:T(8,128)(2,1)S(1)} %copy-done.3), channel_id=1, source_target_pairs={{0,12},{2,14},{4,0},{6,2},{8,4},{10,6},{12,8},{14,10},{1,13},{3,15... | collective-permute-start | bytes 2359304 | tf_op jit(solution)/shard_map/ppermute | solution.py:236
  16.0 0.5 fusion.3.order_ref
  16.5 0.0 copy-start.4
  16.5 31.2 %moments.1.refs_6_.refs_7_.refs_8_.refs_2_.refs_3_ = bf16[8,384,1024]{2,1,0:T(8,128)(2,1)} custom-call(s32[8]{0:T(128)} %fusion.3.order_ref, bf16[384,3584]{1,0:T(8,128)(2,1)} %hidden.1.hidden_ref, s32[3584,4096]{1,0:T(8,128)} %refs_3_.5), custom_call_target="tpu_custom_call" | custom-call | flops 22548578304 | bytes 58720256 | tf_op jit(solution)/shard_map/moments/pallas_call | solution.py:91
  47.7 0.0 collective-permute-done.1.refs_2_
  47.7 0.0 collective-permute-done.refs_0_
  47.7 0.0 collective-permute-done.2.refs_1_
  47.7 0.1 collective-permute-start.6
  47.8 0.4 collective-permute-start.3
  48.1 1.7 %collective-permute-start.5 = (bf16[384,1024]{1,0:T(8,128)(2,1)S(1)}, bf16[384,1024]{1,0:T(8,128)(2,1)S(1)}, u32[]{:S(2)}, u32[]{:S(2)}) collective-permute-start(bf16[384,1024]{1,0:T(8,128)(2,1)S(1)} %collective-permute-done.2.refs_1_), channel_id=1, source_target_pairs={{0,2},{2,0},{4,6},{6,4},{8,10},{10,8},{12,14},{14,12},{1,3},{3,1},... | collective-permute-start | bytes 2359304 | tf_op jit(solution)/shard_map/ppermute | solution.py:236
  49.8 0.0 copy-done.4
  49.8 14.5 %back.2 = (f32[384,3584]{1,0:T(8,128)S(1)}, f32[1,1024]{1,0:T(1,128)S(1)}, f32[1,1024]{1,0:T(1,128)S(1)}, f32[1,1024]{1,0:T(1,128)S(1)}) custom-call(s32[8]{0:T(128)S(1)} %copy-done.4, bf16[384,1024]{1,0:T(8,128)(2,1)S(1)} %collective-permute-done.refs_0_, bf16[384,1024]{1,0:T(8,128)(2,1)S(1)} %collective-permute-done.2.refs_1_, ...), custom_call_target="tpu_custom_call" | custom-call | flops 8455716864 | bytes 22020096 | tf_op jit(solution)/shard_map/back/pallas_call | solution.py:191
  64.4 0.0 copy-start.2
  64.4 2.4 %copy-done.2 = f32[384,3584]{1,0:T(8,128)} copy-done((f32[384,3584]{1,0:T(8,128)}, f32[384,3584]{1,0:T(8,128)S(1)}, u32[]{:S(2)}) %copy-start.2) | copy-done | bytes 5505048
  66.8 1.6 %collective-permute-done.3.refs_2_ = bf16[384,1024]{1,0:T(8,128)(2,1)} collective-permute-done((bf16[384,1024]{1,0:T(8,128)(2,1)S(1)}, bf16[384,1024]{1,0:T(8,128)(2,1)}, u32[]{:S(2)}, u32[]{:S(2)}) %collective-permute-start.3) | collective-permute-done | bytes 786464 | tf_op jit(solution)/shard_map/ppermute | solution.py:236
  68.4 0.0 slice-start
  68.4 1.3 %collective-permute-start.4 = (bf16[384,1024]{1,0:T(8,128)(2,1)}, bf16[384,1024]{1,0:T(8,128)(2,1)S(1)}, u32[]{:S(2)}, u32[]{:S(2)}) collective-permute-start(bf16[384,1024]{1,0:T(8,128)(2,1)} %collective-permute-done.3.refs_2_), channel_id=1, source_target_pairs={{0,4},{2,6},{4,8},{6,10},{8,12},{10,14},{12,0},{14,2},{1,5},{3,7},... | collective-permute-start | bytes 2359304 | tf_op jit(solution)/shard_map/ppermute | solution.py:236
  69.7 0.0 collective-permute-done.6.refs_1_
  69.7 16.3 %back.3 = (f32[384,3584]{1,0:T(8,128)S(1)}, f32[1,1024]{1,0:T(1,128)S(1)}, f32[1,1024]{1,0:T(1,128)S(1)}, f32[1,1024]{1,0:T(1,128)S(1)}) custom-call(s32[8]{0:T(128)S(1)} %copy-done.4, bf16[384,1024]{1,0:T(8,128)(2,1)S(1)} %copy-done.3, bf16[384,1024]{1,0:T(8,128)(2,1)S(1)} %collective-permute-done.6.refs_1_, ...), custom_call_target="tpu_custom_call" | custom-call | flops 8455716864 | bytes 22020096 | tf_op jit(solution)/shard_map/back/pallas_call | solution.py:191
  86.0 0.0 collective-permute-done.5.refs_1_
  86.0 0.8 collective-permute-done.4.refs_0_
  86.7 0.0 slice-done
  86.7 0.0 slice-done.1
  86.8 0.0 copy-start.1
  86.8 0.2 sums.1
  87.0 0.1 collective-permute-start.7
  87.0 0.6 collective-permute-start.8
  87.6 1.2 %collective-permute-start.9 = (f32[4,512]{1,0:T(4,128)S(1)}, f32[4,512]{1,0:T(4,128)S(1)}, u32[]{:S(2)}, u32[]{:S(2)}) collective-permute-start(f32[4,512]{1,0:T(4,128)S(1)} %get-tuple-element.46), channel_id=1, source_target_pairs={{0,3},{1,2},{2,1},{3,0},{4,7},{5,6},{6,5},{7,4},{8,11},{9,10},{10,... | collective-permute-start | bytes 24584 | tf_op jit(solution)/shard_map/ppermute | solution.py:267
  88.9 0.0 collective-permute-done.7
  88.9 1.9 %collective-permute-done.8 = f32[4,512]{1,0:T(4,128)S(1)} collective-permute-done((f32[4,512]{1,0:T(4,128)S(1)}, f32[4,512]{1,0:T(4,128)S(1)}, u32[]{:S(2)}, u32[]{:S(2)}) %collective-permute-start.8) | collective-permute-done | bytes 8224 | tf_op jit(solution)/shard_map/ppermute | solution.py:236
  90.8 0.0 collective-permute-done.9
  90.8 2.1 %collective-permute-start.10 = (f32[1,512]{1,0:T(1,128)S(1)}, f32[1,512]{1,0:T(1,128)S(1)}, u32[]{:S(2)}, u32[]{:S(2)}) collective-permute-start(f32[1,512]{1,0:T(1,128)S(1)} %get-tuple-element.47), channel_id=1, source_target_pairs={{0,12},{2,14},{4,0},{6,2},{8,4},{10,6},{12,8},{14,10},{1,13},{3,15... | collective-permute-start | bytes 6152 | tf_op jit(solution)/shard_map/ppermute | solution.py:236
  92.9 0.0 collective-permute-start.12
  92.9 2.2 %collective-permute-start.11 = (f32[1,512]{1,0:T(1,128)S(1)}, f32[1,512]{1,0:T(1,128)S(1)}, u32[]{:S(2)}, u32[]{:S(2)}) collective-permute-start(f32[1,512]{1,0:T(1,128)S(1)} %get-tuple-element.49), channel_id=1, source_target_pairs={{0,8},{2,10},{4,12},{6,14},{8,0},{10,2},{12,4},{14,6},{1,9},{3,11}... | collective-permute-start | bytes 6152 | tf_op jit(solution)/shard_map/ppermute | solution.py:236
  95.2 0.0 copy-done
  95.2 0.0 copy-done.1
  95.2 13.7 %tail.1 = (bf16[384,3584]{1,0:T(8,128)(2,1)}, bf16[384,3584]{1,0:T(8,128)(2,1)}) custom-call(s32[8]{0:T(128)S(1)} %copy-done.4, bf16[384,1024]{1,0:T(8,128)(2,1)S(1)} %collective-permute-done.4.refs_0_, bf16[384,1024]{1,0:T(8,128)(2,1)S(1)} %collective-permute-done.5.refs_1_, s32[3584,4096]{1,0:T(8,128)} %refs_3_.5, s32[3584,4096]{1,0:T(8,128)} %refs_3_.5, ...), custom_call_target="tpu_custom_call" | custom-call | flops 5637144576 | bytes 14680064 | tf_op jit(solution)/shard_map/tail/pallas_call | solution.py:191
  108.9 0.0 collective-permute-done.10
  108.9 0.0 collective-permute-done.12
  108.9 0.0 collective-permute-done.11
  109.0 0.1 copy.8
  109.1 0.7 reshape.21
  (7 shorter events, 0.1 us)
Async XLA Ops:
  3.0 10.7 %copy-start.3 = (bf16[384,1024]{1,0:T(8,128)(2,1)S(1)}, bf16[384,1024]{1,0:T(8,128)(2,1)}, u32[]{:S(2)}) copy-start(bf16[384,1024]{1,0:T(8,128)(2,1)} %scale.1.refs_0_) | copy-start | bytes 2359300
  3.0 44.6 %collective-permute-start.1 = (bf16[384,1024]{1,0:T(8,128)(2,1)}, bf16[384,1024]{1,0:T(8,128)(2,1)S(1)}, u32[]{:S(2)}, u32[]{:S(2)}) collective-permute-start(bf16[384,1024]{1,0:T(8,128)(2,1)} %scale.1.refs_0_), channel_id=1, source_target_pairs={{0,2},{2,0},{4,6},{6,4},{8,10},{10,8},{12,14},{14,12},{1,3},{3,1},... | collective-permute-start | bytes 2359304 | tf_op jit(solution)/shard_map/ppermute | solution.py:236
  6.0 41.7 %collective-permute-start = (bf16[384,1024]{1,0:T(8,128)(2,1)}, bf16[384,1024]{1,0:T(8,128)(2,1)S(1)}, u32[]{:S(2)}, u32[]{:S(2)}) collective-permute-start(bf16[384,1024]{1,0:T(8,128)(2,1)} %scale.1.refs_0_), channel_id=1, source_target_pairs={{0,4},{2,6},{4,8},{6,10},{8,12},{10,14},{12,0},{14,2},{1,5},{3,7},... | collective-permute-start | bytes 2359304 | tf_op jit(solution)/shard_map/ppermute | solution.py:236
  13.7 33.9 %collective-permute-start.2 = (bf16[384,1024]{1,0:T(8,128)(2,1)S(1)}, bf16[384,1024]{1,0:T(8,128)(2,1)S(1)}, u32[]{:S(2)}, u32[]{:S(2)}) collective-permute-start(bf16[384,1024]{1,0:T(8,128)(2,1)S(1)} %copy-done.3), channel_id=1, source_target_pairs={{0,12},{2,14},{4,0},{6,2},{8,4},{10,6},{12,8},{14,10},{1,13},{3,15... | collective-permute-start | bytes 2359304 | tf_op jit(solution)/shard_map/ppermute | solution.py:236
  16.5 33.3 %copy-start.4 = (s32[8]{0:T(128)S(1)}, s32[8]{0:T(128)}, u32[]{:S(2)}) copy-start(s32[8]{0:T(128)} %fusion.3.order_ref) | copy-start | bytes 100
  47.7 22.0 %collective-permute-start.6 = (bf16[384,1024]{1,0:T(8,128)(2,1)S(1)}, bf16[384,1024]{1,0:T(8,128)(2,1)S(1)}, u32[]{:S(2)}, u32[]{:S(2)}) collective-permute-start(bf16[384,1024]{1,0:T(8,128)(2,1)S(1)} %collective-permute-done.refs_0_), channel_id=1, source_target_pairs={{0,4},{2,6},{4,8},{6,10},{8,12},{10,14},{12,0},{14,2},{1,5},{3,7},... | collective-permute-start | bytes 2359304 | tf_op jit(solution)/shard_map/ppermute | solution.py:236
  47.8 20.7 %collective-permute-start.3 = (bf16[384,1024]{1,0:T(8,128)(2,1)S(1)}, bf16[384,1024]{1,0:T(8,128)(2,1)}, u32[]{:S(2)}, u32[]{:S(2)}) collective-permute-start(bf16[384,1024]{1,0:T(8,128)(2,1)S(1)} %collective-permute-done.refs_0_), channel_id=1, source_target_pairs={{0,2},{2,0},{4,6},{6,4},{8,10},{10,8},{12,14},{14,12},{1,3},{3,1},... | collective-permute-start | bytes 2359304 | tf_op jit(solution)/shard_map/ppermute | solution.py:236
  48.1 37.9 %collective-permute-start.5 = (bf16[384,1024]{1,0:T(8,128)(2,1)S(1)}, bf16[384,1024]{1,0:T(8,128)(2,1)S(1)}, u32[]{:S(2)}, u32[]{:S(2)}) collective-permute-start(bf16[384,1024]{1,0:T(8,128)(2,1)S(1)} %collective-permute-done.2.refs_1_), channel_id=1, source_target_pairs={{0,2},{2,0},{4,6},{6,4},{8,10},{10,8},{12,14},{14,12},{1,3},{3,1},... | collective-permute-start | bytes 2359304 | tf_op jit(solution)/shard_map/ppermute | solution.py:236
  64.4 2.4 %copy-start.2 = (f32[384,3584]{1,0:T(8,128)}, f32[384,3584]{1,0:T(8,128)S(1)}, u32[]{:S(2)}) copy-start(f32[384,3584]{1,0:T(8,128)S(1)} %get-tuple-element.33.refs_9_) | copy-start | bytes 16515076
  68.4 18.3 %slice-start = ((s8[6291456]{0:T(1024)(128)(4,1)}), s8[4194304]{0:T(1024)(128)(4,1)S(1)}, s32[]{:S(2)}) async-start(s8[6291456]{0:T(1024)(128)(4,1)} %bitcast.3), calls=%async_computation | async-start | bytes 8388608
  68.4 18.3 %slice-start.1 = ((s8[6291456]{0:T(1024)(128)(4,1)}), s8[2097152]{0:T(1024)(128)(4,1)S(1)}, s32[]{:S(2)}) async-start(s8[6291456]{0:T(1024)(128)(4,1)} %bitcast.3), calls=%async_computation.1 | async-start | bytes 4194304
  68.4 18.3 %collective-permute-start.4 = (bf16[384,1024]{1,0:T(8,128)(2,1)}, bf16[384,1024]{1,0:T(8,128)(2,1)S(1)}, u32[]{:S(2)}, u32[]{:S(2)}) collective-permute-start(bf16[384,1024]{1,0:T(8,128)(2,1)} %collective-permute-done.3.refs_2_), channel_id=1, source_target_pairs={{0,4},{2,6},{4,8},{6,10},{8,12},{10,14},{12,0},{14,2},{1,5},{3,7},... | collective-permute-start | bytes 2359304 | tf_op jit(solution)/shard_map/ppermute | solution.py:236
  86.7 8.4 %copy-start = (bf16[384,3584]{1,0:T(8,128)(2,1)S(1)}, bf16[384,3584]{1,0:T(8,128)(2,1)}, u32[]{:S(2)}) copy-start(bf16[384,3584]{1,0:T(8,128)(2,1)} %refs_5_.5) | copy-start | bytes 8257540
  86.8 8.4 %copy-start.1 = (bf16[384,3584]{1,0:T(8,128)(2,1)S(1)}, bf16[384,3584]{1,0:T(8,128)(2,1)}, u32[]{:S(2)}) copy-start(bf16[384,3584]{1,0:T(8,128)(2,1)} %refs_6_.1) | copy-start | bytes 8257540
  87.0 1.9 %collective-permute-start.7 = (f32[4,512]{1,0:T(4,128)S(1)}, f32[4,512]{1,0:T(4,128)S(1)}, u32[]{:S(2)}, u32[]{:S(2)}) collective-permute-start(f32[4,512]{1,0:T(4,128)S(1)} %get-tuple-element.44), channel_id=1, source_target_pairs={{0,1},{1,0},{2,3},{3,2},{4,5},{5,4},{6,7},{7,6},{8,9},{9,8},{10,11... | collective-permute-start | bytes 24584 | tf_op jit(solution)/shard_map/ppermute | solution.py:266
  87.0 3.8 %collective-permute-start.8 = (f32[4,512]{1,0:T(4,128)S(1)}, f32[4,512]{1,0:T(4,128)S(1)}, u32[]{:S(2)}, u32[]{:S(2)}) collective-permute-start(f32[4,512]{1,0:T(4,128)S(1)} %get-tuple-element.45), channel_id=1, source_target_pairs={{0,2},{2,0},{4,6},{6,4},{8,10},{10,8},{12,14},{14,12},{1,3},{3,1},... | collective-permute-start | bytes 24584 | tf_op jit(solution)/shard_map/ppermute | solution.py:236
  87.6 3.2 %collective-permute-start.9 = (f32[4,512]{1,0:T(4,128)S(1)}, f32[4,512]{1,0:T(4,128)S(1)}, u32[]{:S(2)}, u32[]{:S(2)}) collective-permute-start(f32[4,512]{1,0:T(4,128)S(1)} %get-tuple-element.46), channel_id=1, source_target_pairs={{0,3},{1,2},{2,1},{3,0},{4,7},{5,6},{6,5},{7,4},{8,11},{9,10},{10,... | collective-permute-start | bytes 24584 | tf_op jit(solution)/shard_map/ppermute | solution.py:267
  90.8 18.1 %collective-permute-start.10 = (f32[1,512]{1,0:T(1,128)S(1)}, f32[1,512]{1,0:T(1,128)S(1)}, u32[]{:S(2)}, u32[]{:S(2)}) collective-permute-start(f32[1,512]{1,0:T(1,128)S(1)} %get-tuple-element.47), channel_id=1, source_target_pairs={{0,12},{2,14},{4,0},{6,2},{8,4},{10,6},{12,8},{14,10},{1,13},{3,15... | collective-permute-start | bytes 6152 | tf_op jit(solution)/shard_map/ppermute | solution.py:236
  92.9 16.0 %collective-permute-start.12 = (f32[1,512]{1,0:T(1,128)S(1)}, f32[1,512]{1,0:T(1,128)S(1)}, u32[]{:S(2)}, u32[]{:S(2)}) collective-permute-start(f32[1,512]{1,0:T(1,128)S(1)} %get-tuple-element.48), channel_id=1, source_target_pairs={{0,4},{2,6},{4,8},{6,10},{8,12},{10,14},{12,0},{14,2},{1,5},{3,7},... | collective-permute-start | bytes 6152 | tf_op jit(solution)/shard_map/ppermute | solution.py:236
  92.9 16.0 %collective-permute-start.11 = (f32[1,512]{1,0:T(1,128)S(1)}, f32[1,512]{1,0:T(1,128)S(1)}, u32[]{:S(2)}, u32[]{:S(2)}) collective-permute-start(f32[1,512]{1,0:T(1,128)S(1)} %get-tuple-element.49), channel_id=1, source_target_pairs={{0,8},{2,10},{4,12},{6,14},{8,0},{10,2},{12,4},{14,6},{1,9},{3,11}... | collective-permute-start | bytes 6152 | tf_op jit(solution)/shard_map/ppermute | solution.py:236
